TPU v7x, 256 devices: a whole 4x4x8 slice. The times are simulated.
256 devices in a mesh: dp: 32 (over z, x), mp: 8 (over y, core).
Axes of the slice: x: 4, y: 4, z: 8, core: 2. Of those that a mesh axis runs over, the one named last changes fastest.
Arguments:
- queries: bfloat16 [4096, 8192], P('dp', 'mp'), may hold values from -8 to 8
- grad_out: bfloat16 [4096, 8192], P('dp', 'mp'), may hold values from -6 to 6
- row_dest: int32 [4096], P('dp'), may hold values from 0 to 31, as said below
- row_slot: int32 [4096], P('dp'), may hold values from 0 to 127, as said below
- block_image: int32 [128], P('dp'), may hold values from 0 to 31, as said below
- image_owner: int32 [32], replicated, may hold values from 0 to 31, as said below
- image_tiles: int32 [32], P('dp'), may hold values from 1 to 4, as said below
- img_keys: bfloat16 [32, 6656, 1024], P('dp', None, 'mp'), may hold values from -8 to 8
- img_values: bfloat16 [32, 6656, 1024], P('dp', None, 'mp'), may hold values from -6 to 6
Outputs:
- attended: bfloat16 [4096, 8192], P('dp', 'mp')
- grad_queries: bfloat16 [4096, 8192], P('dp', 'mp')
- grad_keys: bfloat16 [32, 6656, 1024], P('dp', None, 'mp')
- grad_values: bfloat16 [32, 6656, 1024], P('dp', None, 'mp')
Inputs may be any that keep to these rules, and one draw needn't show every extreme that they name: `row_dest`: one index of dp sends at most 8 rows to any one index, exactly 8 to some; every index receives exactly 128 rows; the row counts that an index sends to the others are the same numbers on every index, assigned to other destinations. `row_slot`: the rows assigned to one index take distinct positions. `block_image`: block b lies on index b // 4 of dp and cites an image held by that index or by the next one (index + 1, modulo the axis); on every index one or two blocks cite the next one; every image is cited by at most 5 blocks, and some image by exactly so many. `image_owner`: A permutation of the indices of dp. `image_tiles`: some image has 4 tiles.
All inputs are finite; a program needn't handle non-finite values.
Results may differ from a plain program's by a relative error of at most 0.015.
Values may be sent and summed in bfloat16 or wider, within the bound.
A program may use at most 128 MiB of HBM per device.

v0:
```python
import jax
import jax.numpy as jnp
from jax import lax
from jax.sharding import PartitionSpec as P

HD = 128
TILE_TOK = 1601
TOKP = 1664
TB = 32
KEYS = 6656
GROUP = 8


def passed_along(shard, axis, by):
    count = lax.axis_size(axis)
    return lax.ppermute(shard, axis, [(i, (i + by) % count) for i in range(count)])


def head_pass(query_rows, grad_rows, key_rows, value_rows, valid_keys):
    score_scale = HD ** (-0.5)
    scores = (
        lax.dot_general(
            query_rows, key_rows, (((1,), (1,)), ((), ())), preferred_element_type=jnp.float32
        )
        * score_scale
    )
    masked = jnp.where(valid_keys[None, :], scores, -jnp.inf)
    top_score = jnp.max(masked, axis=1, keepdims=True)
    weights = jnp.where(valid_keys[None, :], jnp.exp(scores - top_score), 0.0)
    probs = weights / jnp.sum(weights, axis=1, keepdims=True)
    probs_low = probs.astype(jnp.bfloat16)
    attended = jnp.dot(probs_low, value_rows, preferred_element_type=jnp.float32)
    grad_value = lax.dot_general(
        probs_low, grad_rows, (((0,), (0,)), ((), ())), preferred_element_type=jnp.float32
    )
    grad_probs = lax.dot_general(
        grad_rows, value_rows, (((1,), (1,)), ((), ())), preferred_element_type=jnp.float32
    )
    row_delta = jnp.sum(grad_rows.astype(jnp.float32) * attended, axis=1, keepdims=True)
    grad_scores = (probs * (grad_probs - row_delta) * score_scale).astype(jnp.bfloat16)
    grad_query = jnp.dot(grad_scores, key_rows, preferred_element_type=jnp.float32)
    grad_key = lax.dot_general(
        grad_scores, query_rows, (((0,), (0,)), ((), ())), preferred_element_type=jnp.float32
    )
    return (attended, grad_query, grad_key, grad_value)


def block_pass(query_block, grad_block, key_block, value_block, tile_count):
    local_heads = key_block.shape[1] // HD
    block_rows = query_block.shape[0]
    query_heads = (
        query_block.reshape(block_rows, local_heads, GROUP, HD)
        .transpose(1, 0, 2, 3)
        .reshape(local_heads, block_rows * GROUP, HD)
    )
    grad_heads = (
        grad_block.reshape(block_rows, local_heads, GROUP, HD)
        .transpose(1, 0, 2, 3)
        .reshape(local_heads, block_rows * GROUP, HD)
    )
    key_heads = key_block.reshape(KEYS, local_heads, HD).transpose(1, 0, 2)
    value_heads = value_block.reshape(KEYS, local_heads, HD).transpose(1, 0, 2)
    positions = jnp.arange(KEYS)
    valid_keys = (positions % TOKP < TILE_TOK) & (positions // TOKP < tile_count)
    out_part, query_part, key_part, value_part = jax.vmap(head_pass, in_axes=(0, 0, 0, 0, None))(
        query_heads, grad_heads, key_heads, value_heads, valid_keys
    )
    out_part = (
        out_part.reshape(local_heads, block_rows, GROUP, HD)
        .transpose(1, 0, 2, 3)
        .reshape(block_rows, -1)
    )
    query_part = (
        query_part.reshape(local_heads, block_rows, GROUP, HD)
        .transpose(1, 0, 2, 3)
        .reshape(block_rows, -1)
    )
    key_part = key_part.transpose(1, 0, 2).reshape(KEYS, -1)
    value_part = value_part.transpose(1, 0, 2).reshape(KEYS, -1)
    return (out_part, query_part, key_part, value_part)


def shards(
    queries,
    grad_out,
    row_dest,
    row_slot,
    block_image,
    image_owner,
    image_tiles,
    img_keys,
    img_values,
):
    ranks = lax.axis_size("dp")
    my_index = lax.axis_index("dp")
    tok_count = queries.shape[0]
    width = queries.shape[1]
    capacity = 2 * tok_count // ranks
    blocks_here = tok_count // TB
    onehot_dest = (row_dest[:, None] == jnp.arange(ranks)[None, :]).astype(jnp.int32)
    earlier = jnp.cumsum(onehot_dest, axis=0) - onehot_dest
    position = jnp.sum(earlier * onehot_dest, axis=1)
    target = row_dest * capacity + position
    send_map = target[None, :] == jnp.arange(ranks * capacity)[:, None]
    send_low = send_map.astype(jnp.bfloat16)
    payload = jnp.concatenate([queries, grad_out], axis=1)
    send_rows = jnp.dot(send_low, payload, preferred_element_type=jnp.float32).astype(jnp.bfloat16)
    send_slots = jnp.sum(jnp.where(send_map, row_slot[None, :] + 1, 0), axis=1)
    got_rows, got_slots = (
        lax.all_to_all(
            send_rows.reshape(ranks, capacity, 2 * width),
            "dp",
            split_axis=0,
            concat_axis=0,
            tiled=True,
        ),
        lax.all_to_all(
            send_slots.reshape(ranks, capacity), "dp", split_axis=0, concat_axis=0, tiled=True
        ),
    )
    place_map = ((got_slots.reshape(-1) - 1)[None, :] == jnp.arange(tok_count)[:, None]).astype(
        jnp.bfloat16
    )
    balanced = jnp.dot(
        place_map, got_rows.reshape(ranks * capacity, 2 * width), preferred_element_type=jnp.float32
    ).astype(jnp.bfloat16)
    query_blocks = balanced[:, :width].reshape(blocks_here, TB, width)
    grad_blocks = balanced[:, width:].reshape(blocks_here, TB, width)
    own_keys = img_keys[0]
    own_values = img_values[0]
    key_width = own_keys.shape[1]
    near_keys, near_values, near_tiles = passed_along((own_keys, own_values, image_tiles), "dp", -1)
    pair_keys = jnp.stack([own_keys, near_keys])
    pair_values = jnp.stack([own_values, near_values])
    pair_tiles = jnp.concatenate([image_tiles, near_tiles])

    def visit_block(block_id, carry):
        key_acc, value_acc, out_store, query_store = carry
        source_rank = (image_owner[block_image[block_id]] - my_index) % ranks
        key_pick = lax.dynamic_index_in_dim(pair_keys, source_rank, 0, keepdims=False)
        value_pick = lax.dynamic_index_in_dim(pair_values, source_rank, 0, keepdims=False)
        out_part, query_part, key_part, value_part = block_pass(
            query_blocks[block_id],
            grad_blocks[block_id],
            key_pick,
            value_pick,
            pair_tiles[source_rank],
        )
        key_acc = key_acc.at[source_rank].add(key_part)
        value_acc = value_acc.at[source_rank].add(value_part)
        out_store = out_store.at[block_id].set(out_part)
        query_store = query_store.at[block_id].set(query_part)
        return (key_acc, value_acc, out_store, query_store)

    start_state = (
        jnp.zeros((2, KEYS, key_width), jnp.float32),
        jnp.zeros((2, KEYS, key_width), jnp.float32),
        jnp.zeros((blocks_here, TB, width), jnp.float32),
        jnp.zeros((blocks_here, TB, width), jnp.float32),
    )
    key_acc, value_acc, out_store, query_store = lax.fori_loop(
        0, blocks_here, visit_block, start_state
    )
    back_keys, back_values = passed_along((key_acc[1], value_acc[1]), "dp", 1)
    grad_keys = (key_acc[0] + back_keys).astype(jnp.bfloat16)[None]
    grad_values = (value_acc[0] + back_values).astype(jnp.bfloat16)[None]
    attended_blocks = out_store.astype(jnp.bfloat16)
    query_grad_blocks = query_store.astype(jnp.bfloat16)
    results = jnp.concatenate(
        [attended_blocks.reshape(tok_count, width), query_grad_blocks.reshape(tok_count, width)],
        axis=1,
    )
    reply = lax.dot_general(
        place_map, results, (((0,), (0,)), ((), ())), preferred_element_type=jnp.float32
    ).astype(jnp.bfloat16)
    returned = lax.all_to_all(
        reply.reshape(ranks, capacity, 2 * width), "dp", split_axis=0, concat_axis=0, tiled=True
    )
    final_rows = lax.dot_general(
        send_low,
        returned.reshape(ranks * capacity, 2 * width),
        (((0,), (0,)), ((), ())),
        preferred_element_type=jnp.float32,
    ).astype(jnp.bfloat16)
    return (final_rows[:, :width], final_rows[:, width:], grad_keys, grad_values)


def solution(mesh):
    return jax.shard_map(
        shards,
        mesh=mesh,
        in_specs=(
            P("dp", "mp"),
            P("dp", "mp"),
            P("dp"),
            P("dp"),
            P("dp"),
            P(),
            P("dp"),
            P("dp", None, "mp"),
            P("dp", None, "mp"),
        ),
        out_specs=(P("dp", "mp"), P("dp", "mp"), P("dp", None, "mp"), P("dp", None, "mp")),
        check_vma=False,
    )
```

profile of v0, /device:TPU:8, one launch (start us, length us, event | category | flops | bytes accessed | tf_op | source)
XLA Modules:
  0.0 502.4 jit_solution(4483447909048391148)
XLA Ops:
  0.6 8.1 %collective-permute-start.1 = (bf16[6656,128]{1,0:T(8,128)(2,1)}, bf16[6656,128]{1,0:T(8,128)(2,1)}, u32[]{:S(2)}, u32[]{:S(2)}) collective-permute-start(bf16[6656,128]{1,0:T(8,128)(2,1)} %bitcast.118), channel_id=1, source_target_pairs={{0,248},{8,0},{16,8},{24,16},{32,24},{40,32},{48,40},{56,48},{64,5... | collective-permute-start | bytes 5111816 | tf_op jit(solution)/shard_map/ppermute | solution.py:16
  12.8 4.2 all-to-all-start
  19.5 62.9 %all-to-all-done = s32[32,1,8]{2,1,0:T(1,128)S(1)} async-done(((s32[32,1,8]{2,1,0:T(1,128)}), s32[32,1,8]{2,1,0:T(1,128)S(1)}, u32[]{:S(2)}, u32[]{:S(2)}) %all-to-all-start) | async-done | bytes 1056 | tf_op jit(solution)/shard_map/all_to_all | solution.py:117
  82.4 9.4 %all-to-all-start.1 = ((bf16[32,8,2048]{2,1,0:T(8,128)(2,1)}), bf16[32,8,2048]{2,1,0:T(8,128)(2,1)S(1)}, u32[]{:S(2)}, u32[]{:S(2)}) async-start(bf16[32,8,2048]{2,1,0:T(8,128)(2,1)} %fusion.39), calls=%async_computation.1 | async-start | bytes 2097152 | tf_op jit(solution)/shard_map/all_to_all | solution.py:110
  91.9 5.3 %collective-permute-start = (s32[1]{0:T(128)}, s32[1]{0:T(128)}, u32[]{:S(2)}, u32[]{:S(2)}) collective-permute-start(s32[1]{0:T(128)} %param.25), channel_id=1, source_target_pairs={{0,248},{8,0},{16,8},{24,16},{32,24},{40,32},{48,40},{56,48},{64,5... | collective-permute-start | bytes 20 | tf_op jit(solution)/shard_map/ppermute | solution.py:16
  97.8 12.2 %collective-permute-done = s32[1]{0:T(128)} collective-permute-done((s32[1]{0:T(128)}, s32[1]{0:T(128)}, u32[]{:S(2)}, u32[]{:S(2)}) %collective-permute-start) | collective-permute-done | bytes 36 | tf_op jit(solution)/shard_map/ppermute | solution.py:16
  111.5 3.6 pad_maximum_fusion
  115.1 3.6 pad_maximum_fusion.1
  119.8 3.3 broadcast.222
  123.1 3.2 broadcast.222.clone
  127.7 188.7 %while.26 = (s32[]{:T(128)}, f32[2,6656,128]{2,1,0:T(8,128)}, f32[2,6656,128]{2,1,0:T(8,128)}, bf16[4,32,1024]{2,1,0:T(8,128)(2,1)}, bf16[4,32,1024]{2,1,0:T(8,1...) while((s32[]{:T(128)}, f32[2,6656,128]{2,1,0:T(8,128)}, ...), condition=%wide.region_9.10_spmd, body=%wide.region_3.9_spmd.sunk | while | flops 2656731904 | bytes 148496016 | solution.py:161
  143.6 8.7 %fusion.94 = f32[2,6656,128]{2,1,0:T(8,128)} fusion(f32[2,6656,128]{2,1,0:T(8,128)} %get-tuple-element.605, s32[]{:T(128)} %select_n.174, bf16[256,128]{1,0:T(8,128)(2,1)S(1)} %reshape.427, pred[]{:T(512)} %and_reduce_fusion.4, f32[256,6656]{1,0:T(8,128)} %copy-done, f32[256]{0:T(256)S(1)} %fusion.91, f32[256]{0:T(256)S(1)} %get-tuple-element.577, ...), kind=kOutput, calls=%fused_computation.12.clone.1 | convolution fusion | flops 444727296 | bytes 13706752 | tf_op jit(solution)/shard_map/while/body/eval_jaxpr/vmap()/dot_general | solution.py:33
  153.0 5.5 %multiply_reduce_fusion.2 = (f32[256]{0:T(256)S(1)}, bf16[256,128]{0,1:T(8,128)(2,1)}) fusion(bf16[256,128]{0,1:T(8,128)(2,1)} %copy.23, bf16[2,6656,128]{2,1,0:T(8,128)(2,1)S(1)} %copy-done.2, s32[]{:T(128)} %select_n.174, f32[256]{0:T(256)S(1)} %fusion.91, f32[256,6656]{1,0:T(8,128)} %copy-done, f32[256]{0:T(256)S(1)} %get-tuple-element.577, ...), kind=kOutput, calls=%fused_computation.31.clone.1 | convolution fusion | flops 443154176 | bytes 8660996 | tf_op jit(solution)/shard_map/while/body/eval_jaxpr/vmap()/dot_general | solution.py:32
  158.8 2.7 fusion.92
  169.4 5.5 %fusion.93 = f32[2,6656,128]{2,1,0:T(8,128)} fusion(f32[2,6656,128]{2,1,0:T(8,128)} %get-tuple-element.604, s32[]{:T(128)} %select_n.174, bf16[256,6656]{1,0:T(8,128)(2,1)S(1)} %fusion.92, bf16[256,128]{1,0:T(8,128)(2,1)S(1)} %reshape.428, pred[]{:T(512)} %and_reduce_fusion.4), kind=kOutput, calls=%fused_computation.9.clone.1 | convolution fusion | flops 437911552 | bytes 10290176 | tf_op jit(solution)/shard_map/while/body/eval_jaxpr/vmap()/dot_general | solution.py:42
  190.7 8.7 %fusion.94 = f32[2,6656,128]{2,1,0:T(8,128)} fusion(f32[2,6656,128]{2,1,0:T(8,128)} %get-tuple-element.605, s32[]{:T(128)} %select_n.174, bf16[256,128]{1,0:T(8,128)(2,1)S(1)} %reshape.427, pred[]{:T(512)} %and_reduce_fusion.4, f32[256,6656]{1,0:T(8,128)} %copy-done, f32[256]{0:T(256)S(1)} %fusion.91, f32[256]{0:T(256)S(1)} %get-tuple-element.577, ...), kind=kOutput, calls=%fused_computation.12.clone.1 | convolution fusion | flops 444727296 | bytes 13706752 | tf_op jit(solution)/shard_map/while/body/eval_jaxpr/vmap()/dot_general | solution.py:33
  200.1 5.5 %multiply_reduce_fusion.2 = (f32[256]{0:T(256)S(1)}, bf16[256,128]{0,1:T(8,128)(2,1)}) fusion(bf16[256,128]{0,1:T(8,128)(2,1)} %copy.23, bf16[2,6656,128]{2,1,0:T(8,128)(2,1)S(1)} %copy-done.2, s32[]{:T(128)} %select_n.174, f32[256]{0:T(256)S(1)} %fusion.91, f32[256,6656]{1,0:T(8,128)} %copy-done, f32[256]{0:T(256)S(1)} %get-tuple-element.577, ...), kind=kOutput, calls=%fused_computation.31.clone.1 | convolution fusion | flops 443154176 | bytes 8660996 | tf_op jit(solution)/shard_map/while/body/eval_jaxpr/vmap()/dot_general | solution.py:32
  216.6 5.5 %fusion.93 = f32[2,6656,128]{2,1,0:T(8,128)} fusion(f32[2,6656,128]{2,1,0:T(8,128)} %get-tuple-element.604, s32[]{:T(128)} %select_n.174, bf16[256,6656]{1,0:T(8,128)(2,1)S(1)} %fusion.92, bf16[256,128]{1,0:T(8,128)(2,1)S(1)} %reshape.428, pred[]{:T(512)} %and_reduce_fusion.4), kind=kOutput, calls=%fused_computation.9.clone.1 | convolution fusion | flops 437911552 | bytes 10290176 | tf_op jit(solution)/shard_map/while/body/eval_jaxpr/vmap()/dot_general | solution.py:42
  237.9 8.7 %fusion.94 = f32[2,6656,128]{2,1,0:T(8,128)} fusion(f32[2,6656,128]{2,1,0:T(8,128)} %get-tuple-element.605, s32[]{:T(128)} %select_n.174, bf16[256,128]{1,0:T(8,128)(2,1)S(1)} %reshape.427, pred[]{:T(512)} %and_reduce_fusion.4, f32[256,6656]{1,0:T(8,128)} %copy-done, f32[256]{0:T(256)S(1)} %fusion.91, f32[256]{0:T(256)S(1)} %get-tuple-element.577, ...), kind=kOutput, calls=%fused_computation.12.clone.1 | convolution fusion | flops 444727296 | bytes 13706752 | tf_op jit(solution)/shard_map/while/body/eval_jaxpr/vmap()/dot_general | solution.py:33
  247.3 5.5 %multiply_reduce_fusion.2 = (f32[256]{0:T(256)S(1)}, bf16[256,128]{0,1:T(8,128)(2,1)}) fusion(bf16[256,128]{0,1:T(8,128)(2,1)} %copy.23, bf16[2,6656,128]{2,1,0:T(8,128)(2,1)S(1)} %copy-done.2, s32[]{:T(128)} %select_n.174, f32[256]{0:T(256)S(1)} %fusion.91, f32[256,6656]{1,0:T(8,128)} %copy-done, f32[256]{0:T(256)S(1)} %get-tuple-element.577, ...), kind=kOutput, calls=%fused_computation.31.clone.1 | convolution fusion | flops 443154176 | bytes 8660996 | tf_op jit(solution)/shard_map/while/body/eval_jaxpr/vmap()/dot_general | solution.py:32
  263.7 5.5 %fusion.93 = f32[2,6656,128]{2,1,0:T(8,128)} fusion(f32[2,6656,128]{2,1,0:T(8,128)} %get-tuple-element.604, s32[]{:T(128)} %select_n.174, bf16[256,6656]{1,0:T(8,128)(2,1)S(1)} %fusion.92, bf16[256,128]{1,0:T(8,128)(2,1)S(1)} %reshape.428, pred[]{:T(512)} %and_reduce_fusion.4), kind=kOutput, calls=%fused_computation.9.clone.1 | convolution fusion | flops 437911552 | bytes 10290176 | tf_op jit(solution)/shard_map/while/body/eval_jaxpr/vmap()/dot_general | solution.py:42
  285.1 8.7 %fusion.94 = f32[2,6656,128]{2,1,0:T(8,128)} fusion(f32[2,6656,128]{2,1,0:T(8,128)} %get-tuple-element.605, s32[]{:T(128)} %select_n.174, bf16[256,128]{1,0:T(8,128)(2,1)S(1)} %reshape.427, pred[]{:T(512)} %and_reduce_fusion.4, f32[256,6656]{1,0:T(8,128)} %copy-done, f32[256]{0:T(256)S(1)} %fusion.91, f32[256]{0:T(256)S(1)} %get-tuple-element.577, ...), kind=kOutput, calls=%fused_computation.12.clone.1 | convolution fusion | flops 444727296 | bytes 13706752 | tf_op jit(solution)/shard_map/while/body/eval_jaxpr/vmap()/dot_general | solution.py:33
  294.5 5.5 %multiply_reduce_fusion.2 = (f32[256]{0:T(256)S(1)}, bf16[256,128]{0,1:T(8,128)(2,1)}) fusion(bf16[256,128]{0,1:T(8,128)(2,1)} %copy.23, bf16[2,6656,128]{2,1,0:T(8,128)(2,1)S(1)} %copy-done.2, s32[]{:T(128)} %select_n.174, f32[256]{0:T(256)S(1)} %fusion.91, f32[256,6656]{1,0:T(8,128)} %copy-done, f32[256]{0:T(256)S(1)} %get-tuple-element.577, ...), kind=kOutput, calls=%fused_computation.31.clone.1 | convolution fusion | flops 443154176 | bytes 8660996 | tf_op jit(solution)/shard_map/while/body/eval_jaxpr/vmap()/dot_general | solution.py:32
  300.4 2.7 fusion.92
  310.9 5.5 %fusion.93 = f32[2,6656,128]{2,1,0:T(8,128)} fusion(f32[2,6656,128]{2,1,0:T(8,128)} %get-tuple-element.604, s32[]{:T(128)} %select_n.174, bf16[256,6656]{1,0:T(8,128)(2,1)S(1)} %fusion.92, bf16[256,128]{1,0:T(8,128)(2,1)S(1)} %reshape.428, pred[]{:T(512)} %and_reduce_fusion.4), kind=kOutput, calls=%fused_computation.9.clone.1 | convolution fusion | flops 437911552 | bytes 10290176 | tf_op jit(solution)/shard_map/while/body/eval_jaxpr/vmap()/dot_general | solution.py:42
  316.4 4.0 slice_bitcast_fusion
  323.6 13.1 %all-to-all-start.2 = ((bf16[32,8,2048]{2,1,0:T(8,128)(2,1)}), bf16[32,8,2048]{2,1,0:T(8,128)(2,1)}, u32[]{:S(2)}, u32[]{:S(2)}) async-start(bf16[32,8,2048]{2,1,0:T(8,128)(2,1)} %fusion.40), calls=%async_computation.2 | async-start | bytes 2097152 | tf_op jit(solution)/shard_map/all_to_all | solution.py:176
  336.7 4.1 slice_bitcast_fusion.1
  342.6 91.1 %all-to-all-done.2 = bf16[32,8,2048]{2,1,0:T(8,128)(2,1)} async-done(((bf16[32,8,2048]{2,1,0:T(8,128)(2,1)}), bf16[32,8,2048]{2,1,0:T(8,128)(2,1)}, u32[]{:S(2)}, u32[]{:S(2)}) %all-to-all-start.2) | async-done | bytes 1048608 | tf_op jit(solution)/shard_map/all_to_all | solution.py:176
  436.1 5.1 %fusion.42 = bf16[1,6656,128]{2,1,0:T(8,128)(2,1)} fusion(f32[6656,128]{1,0:T(8,128)} %collective-permute-done.4, f32[2,6656,128]{2,1,0:T(8,128)} %get-tuple-element.450), kind=kLoop, calls=%fused_computation.72 | loop fusion | flops 1703936 | bytes 8519680 | tf_op jit(solution)/shard_map/broadcast_in_dim | solution.py:166
  441.3 57.7 %collective-permute-done.3 = f32[6656,128]{1,0:T(8,128)} collective-permute-done((f32[6656,128]{1,0:T(8,128)}, f32[6656,128]{1,0:T(8,128)}, u32[]{:S(2)}, u32[]{:S(2)}) %collective-permute-start.3) | collective-permute-done | bytes 3407904 | tf_op jit(solution)/shard_map/ppermute | solution.py:16
  498.9 3.5 fusion.41
  (159 shorter events, 111.1 us)
Async XLA Ops:
  0.6 110.8 %copy-start.6 = (bf16[1,6656,128]{2,1,0:T(8,128)(2,1)S(1)}, bf16[1,6656,128]{2,1,0:T(8,128)(2,1)}, u32[]{:S(2)}) copy-start(bf16[1,6656,128]{2,1,0:T(8,128)(2,1)} %param.26) | copy-start | bytes 5111812
  0.6 110.8 %collective-permute-start.1 = (bf16[6656,128]{1,0:T(8,128)(2,1)}, bf16[6656,128]{1,0:T(8,128)(2,1)}, u32[]{:S(2)}, u32[]{:S(2)}) collective-permute-start(bf16[6656,128]{1,0:T(8,128)(2,1)} %bitcast.118), channel_id=1, source_target_pairs={{0,248},{8,0},{16,8},{24,16},{32,24},{40,32},{48,40},{56,48},{64,5... | collective-permute-start | bytes 5111816 | tf_op jit(solution)/shard_map/ppermute | solution.py:16
  8.8 106.3 %collective-permute-start.2 = (bf16[6656,128]{1,0:T(8,128)(2,1)}, bf16[6656,128]{1,0:T(8,128)(2,1)}, u32[]{:S(2)}, u32[]{:S(2)}) collective-permute-start(bf16[6656,128]{1,0:T(8,128)(2,1)} %bitcast.119), channel_id=1, source_target_pairs={{0,248},{8,0},{16,8},{24,16},{32,24},{40,32},{48,40},{56,48},{64,5... | collective-permute-start | bytes 5111816 | tf_op jit(solution)/shard_map/ppermute | solution.py:16
  12.0 70.4 %copy-start.11 = (s32[128]{0:T(128)}, s32[128]{0:T(128)S(1)}, u32[]{:S(2)}) copy-start(s32[128]{0:T(128)S(1)} %get-tuple-element.487) | copy-start | bytes 1540
  12.8 69.6 %all-to-all-start = ((s32[32,1,8]{2,1,0:T(1,128)}), s32[32,1,8]{2,1,0:T(1,128)S(1)}, u32[]{:S(2)}, u32[]{:S(2)}) async-start(s32[32,1,8]{2,1,0:T(1,128)} %bitcast.9), calls=%async_computation | async-start | bytes 32768 | tf_op jit(solution)/shard_map/all_to_all | solution.py:117
  82.4 36.3 %all-to-all-start.1 = ((bf16[32,8,2048]{2,1,0:T(8,128)(2,1)}), bf16[32,8,2048]{2,1,0:T(8,128)(2,1)S(1)}, u32[]{:S(2)}, u32[]{:S(2)}) async-start(bf16[32,8,2048]{2,1,0:T(8,128)(2,1)} %fusion.39), calls=%async_computation.1 | async-start | bytes 2097152 | tf_op jit(solution)/shard_map/all_to_all | solution.py:110
  91.9 18.2 %collective-permute-start = (s32[1]{0:T(128)}, s32[1]{0:T(128)}, u32[]{:S(2)}, u32[]{:S(2)}) collective-permute-start(s32[1]{0:T(128)} %param.25), channel_id=1, source_target_pairs={{0,248},{8,0},{16,8},{24,16},{32,24},{40,32},{48,40},{56,48},{64,5... | collective-permute-start | bytes 20 | tf_op jit(solution)/shard_map/ppermute | solution.py:16
  111.4 7.3 %copy-start.9 = (s32[256]{0:T(256)}, s32[256]{0:T(256)S(1)}, u32[]{:S(2)}) copy-start(s32[256]{0:T(256)S(1)} %sub.78) | copy-start | bytes 3076
  143.6 9.4 %copy-start.2 = (bf16[2,6656,128]{2,1,0:T(8,128)(2,1)S(1)}, bf16[2,6656,128]{2,1,0:T(8,128)(2,1)}, u32[]{:S(2)}) copy-start(bf16[2,6656,128]{2,1,0:T(8,128)(2,1)} %get-tuple-element.636) | copy-start | bytes 10223620 | tf_op jit(solution)/shard_map/while
  153.0 5.6 %copy-start.1 = (f32[256,6656]{1,0:T(8,128)S(1)}, f32[256,6656]{1,0:T(8,128)}, u32[]{:S(2)}) copy-start(f32[256,6656]{1,0:T(8,128)} %copy-done) | copy-start | bytes 20447236 | tf_op jit(solution)/shard_map/while
  153.0 5.9 %copy-start.3 = (bf16[2,6656,128]{2,1,0:T(8,128)(2,1)S(1)}, bf16[2,6656,128]{2,1,0:T(8,128)(2,1)}, u32[]{:S(2)}) copy-start(bf16[2,6656,128]{2,1,0:T(8,128)(2,1)} %get-tuple-element.636) | copy-start | bytes 10223620 | tf_op jit(solution)/shard_map/while
  161.5 4.8 copy-start.8
  190.7 9.4 %copy-start.2 = (bf16[2,6656,128]{2,1,0:T(8,128)(2,1)S(1)}, bf16[2,6656,128]{2,1,0:T(8,128)(2,1)}, u32[]{:S(2)}) copy-start(bf16[2,6656,128]{2,1,0:T(8,128)(2,1)} %get-tuple-element.636) | copy-start | bytes 10223620 | tf_op jit(solution)/shard_map/while
  200.1 5.6 %copy-start.1 = (f32[256,6656]{1,0:T(8,128)S(1)}, f32[256,6656]{1,0:T(8,128)}, u32[]{:S(2)}) copy-start(f32[256,6656]{1,0:T(8,128)} %copy-done) | copy-start | bytes 20447236 | tf_op jit(solution)/shard_map/while
  200.1 5.9 %copy-start.3 = (bf16[2,6656,128]{2,1,0:T(8,128)(2,1)S(1)}, bf16[2,6656,128]{2,1,0:T(8,128)(2,1)}, u32[]{:S(2)}) copy-start(bf16[2,6656,128]{2,1,0:T(8,128)(2,1)} %get-tuple-element.636) | copy-start | bytes 10223620 | tf_op jit(solution)/shard_map/while
  208.6 4.8 copy-start.8
  237.9 9.4 %copy-start.2 = (bf16[2,6656,128]{2,1,0:T(8,128)(2,1)S(1)}, bf16[2,6656,128]{2,1,0:T(8,128)(2,1)}, u32[]{:S(2)}) copy-start(bf16[2,6656,128]{2,1,0:T(8,128)(2,1)} %get-tuple-element.636) | copy-start | bytes 10223620 | tf_op jit(solution)/shard_map/while
  247.3 5.6 %copy-start.1 = (f32[256,6656]{1,0:T(8,128)S(1)}, f32[256,6656]{1,0:T(8,128)}, u32[]{:S(2)}) copy-start(f32[256,6656]{1,0:T(8,128)} %copy-done) | copy-start | bytes 20447236 | tf_op jit(solution)/shard_map/while
  247.3 5.9 %copy-start.3 = (bf16[2,6656,128]{2,1,0:T(8,128)(2,1)S(1)}, bf16[2,6656,128]{2,1,0:T(8,128)(2,1)}, u32[]{:S(2)}) copy-start(bf16[2,6656,128]{2,1,0:T(8,128)(2,1)} %get-tuple-element.636) | copy-start | bytes 10223620 | tf_op jit(solution)/shard_map/while
  255.8 4.8 copy-start.8
  285.1 9.4 %copy-start.2 = (bf16[2,6656,128]{2,1,0:T(8,128)(2,1)S(1)}, bf16[2,6656,128]{2,1,0:T(8,128)(2,1)}, u32[]{:S(2)}) copy-start(bf16[2,6656,128]{2,1,0:T(8,128)(2,1)} %get-tuple-element.636) | copy-start | bytes 10223620 | tf_op jit(solution)/shard_map/while
  294.5 5.6 %copy-start.1 = (f32[256,6656]{1,0:T(8,128)S(1)}, f32[256,6656]{1,0:T(8,128)}, u32[]{:S(2)}) copy-start(f32[256,6656]{1,0:T(8,128)} %copy-done) | copy-start | bytes 20447236 | tf_op jit(solution)/shard_map/while
  294.5 5.9 %copy-start.3 = (bf16[2,6656,128]{2,1,0:T(8,128)(2,1)S(1)}, bf16[2,6656,128]{2,1,0:T(8,128)(2,1)}, u32[]{:S(2)}) copy-start(bf16[2,6656,128]{2,1,0:T(8,128)(2,1)} %get-tuple-element.636) | copy-start | bytes 10223620 | tf_op jit(solution)/shard_map/while
  316.4 5.8 %copy-start.4 = (bf16[4,32,1024]{2,1,0:T(8,128)(2,1)S(1)}, bf16[4,32,1024]{2,1,0:T(8,128)(2,1)}, u32[]{:S(2)}) copy-start(bf16[4,32,1024]{2,1,0:T(8,128)(2,1)} %get-tuple-element.447) | copy-start | bytes 786436
  316.4 5.8 %copy-start.5 = (bf16[4,32,1024]{2,1,0:T(8,128)(2,1)S(1)}, bf16[4,32,1024]{2,1,0:T(8,128)(2,1)}, u32[]{:S(2)}) copy-start(bf16[4,32,1024]{2,1,0:T(8,128)(2,1)} %get-tuple-element.448) | copy-start | bytes 786436
  316.4 5.8 %copy-start.10 = (s32[256]{0:T(256)S(1)}, s32[256]{0:T(256)}, u32[]{:S(2)}) copy-start(s32[256]{0:T(256)} %copy-done.9) | copy-start | bytes 3076
  320.4 115.7 %collective-permute-start.4 = (f32[6656,128]{1,0:T(8,128)}, f32[6656,128]{1,0:T(8,128)}, u32[]{:S(2)}, u32[]{:S(2)}) collective-permute-start(f32[6656,128]{1,0:T(8,128)} %slice_bitcast_fusion), channel_id=1, source_target_pairs={{0,8},{8,16},{16,24},{24,32},{32,40},{40,48},{48,56},{56,64},{64,7... | collective-permute-start | bytes 10223624 | tf_op jit(solution)/shard_map/ppermute | solution.py:16
  323.6 110.1 %all-to-all-start.2 = ((bf16[32,8,2048]{2,1,0:T(8,128)(2,1)}), bf16[32,8,2048]{2,1,0:T(8,128)(2,1)}, u32[]{:S(2)}, u32[]{:S(2)}) async-start(bf16[32,8,2048]{2,1,0:T(8,128)(2,1)} %fusion.40), calls=%async_computation.2 | async-start | bytes 2097152 | tf_op jit(solution)/shard_map/all_to_all | solution.py:176
  336.7 97.0 %copy-start.12 = (s32[128]{0:T(128)S(1)}, s32[128]{0:T(128)}, u32[]{:S(2)}) copy-start(s32[128]{0:T(128)} %copy-done.11) | copy-start | bytes 1540
  336.7 162.2 %slice-start = ((s8[6815744]{0:T(1024)(128)(4,1)}), s8[2621440]{0:T(1024)(128)(4,1)S(1)}, s32[]{:S(2)}) async-start(s8[6815744]{0:T(1024)(128)(4,1)} %bitcast.114), calls=%async_computation.3 | async-start | bytes 5242880
  340.9 158.1 %collective-permute-start.3 = (f32[6656,128]{1,0:T(8,128)}, f32[6656,128]{1,0:T(8,128)}, u32[]{:S(2)}, u32[]{:S(2)}) collective-permute-start(f32[6656,128]{1,0:T(8,128)} %slice_bitcast_fusion.1), channel_id=1, source_target_pairs={{0,8},{8,16},{16,24},{24,32},{32,40},{40,48},{48,56},{56,64},{64,7... | collective-permute-start | bytes 10223624 | tf_op jit(solution)/shard_map/ppermute | solution.py:16
  435.3 63.6 %slice-start.1 = ((s8[6815744]{0:T(1024)(128)(4,1)}), s8[4194304]{0:T(1024)(128)(4,1)S(1)}, s32[]{:S(2)}) async-start(s8[6815744]{0:T(1024)(128)(4,1)} %bitcast.114), calls=%async_computation.4 | async-start | bytes 8388608
  (6 other events, 19.7 us)
where the time goes:
time: 508 us; the launch traced here: 502 us
  waiting for transfers between devices  224 us (44%)
  matrix products  116 us (23%)
  local copies, waits for them, and re-layouts  59.6 us (12%)
  other arithmetic  46.2 us (9%)
  starting transfers between devices  44.5 us (9%)
  loops' own time  11.3 us (2%)
    all_to_all x1, waiting for transfers between devices, shards(): lax.all_to_all(reply.reshape(ranks, capacity, 2 * width), 'dp', split_axi...  91.1 us
    ppermute x5, waiting for transfers between devices, passed_along(): lax.ppermute(shard, axis, [(i, (i + by) % count) for i in range(count)])  69.9 us
    all_to_all x1, waiting for transfers between devices, shards(): lax.all_to_all(send_slots.reshape(ranks, capacity), 'dp', split_axis=0, c...  62.9 us
    dot_general x4, matrix products, head_pass(): lax.dot_general(probs_low, grad_rows, (((0,), (0,)), ((), ())), preferred...  34.6 us
    dot_general x4, matrix products, head_pass(): jnp.dot(probs_low, value_rows, preferred_element_type=jnp.float32)  22.2 us
    dot_general x4, matrix products, head_pass(): lax.dot_general(grad_scores, query_rows, (((0,), (0,)), ((), ())), prefer...  22 us
    ppermute x5, starting transfers between devices, passed_along(): lax.ppermute(shard, axis, [(i, (i + by) % count) for i in range(count)])  17.7 us
    another operation x24, local copies, waits for them, and re-layouts  16.5 us
  transfers between devices with their start and end apart: 8, of which 4 were waited for; matrix products, arithmetic and copies ran while one was open for 5% of the time, Pallas kernels for 0%

commit v1 on v0

v1 whole, which is shorter than its diff:
```python
import functools

import jax
import jax.numpy as jnp
from jax import lax
from jax.experimental import pallas as pl
from jax.experimental.pallas import tpu as pltpu
from jax.sharding import PartitionSpec as P

HD = 128
TILE_TOK = 1601
TOKP = 1664
KEYS = 6656
SCALE = HD**-0.5
LOG2E = 1.4426950408889634
RANKS = 32
CHUNKS = 4
WIDTH = 256
SLAB = 16
SLABS = RANKS * SLAB
OWN = 96
FAR = 64
BAL = 2 * (OWN + FAR)
ROWS = 2 * (OWN + FAR)
STEP = 3328
STEPS = KEYS // STEP
MESH = pl.DeviceIdType.MESH
f32 = jnp.float32
bf16 = jnp.bfloat16
NT = ((1,), (1,))
NN = ((1,), (0,))


def dot(a, b, dims=NN):
    return lax.dot_general(a, b, (dims, ((), ())), preferred_element_type=f32)


def iota(shape, dim):
    return lax.broadcasted_iota(jnp.int32, shape, dim)


def fold(x, op):
    r = x[:, :HD]
    for i in range(1, x.shape[1] // HD):
        r = op(r, x[:, i * HD : (i + 1) * HD])
    return r


def as_column(row, n):
    return jnp.transpose(jnp.broadcast_to(row, (HD, n)))[:, :1]


def kernel(
    image_ref, owner_ref, tiles_ref, dest_ref, slot_ref, q_ref, g_ref, k_ref, v_ref,
    att_ref, gq_ref, gk_ref, gv_ref,
    snd, rcv, rep, ret, tab, tab_in, bal, far, res, back,
    pack, unpack, place, unplace, scores, weights, gk_t, gv_t,
    in_send, in_recv, tab_send, tab_recv, far_send, far_recv, back_send, back_recv, out_send, out_recv,
):
    me = lax.axis_index("dp")
    mz, mx = me // 4, me % 4

    def ahead(k):
        return {"dp": ((mz + k // 4) % 8) * 4 + (mx + k % 4) % 4}

    def behind(k):
        return {"dp": ((mz + 8 - k // 4) % 8) * 4 + (mx + 4 - k % 4) % 4}

    nxt = {"dp": (me + 1) % RANKS}
    prv = {"dp": (me + RANKS - 1) % RANKS}
    barrier = pltpu.get_barrier_semaphore()

    @pl.loop(1, RANKS)
    def _(k):
        pl.semaphore_signal(barrier, 1, device_id=ahead(k), device_id_type=MESH)

    dest = dest_ref[...]
    slot = slot_ref[...]
    offset = (((dest >> 2) - mz) & 7) * 4 + (((dest & 3) - mx) & 3)
    dest_c = as_column(dest, HD)
    same = (dest_c == dest) & (iota((HD, HD), 0) < iota((HD, HD), 1))
    position = jnp.sum(same.astype(jnp.int32), axis=0, keepdims=True)
    target = jnp.concatenate([offset * SLAB + position, offset * SLAB + 8 + position], axis=1)
    pack[...] = (iota((SLABS, 2 * HD), 0) == target).astype(bf16)
    unpack[...] = (as_column(target, 2 * HD) == iota((2 * HD, SLABS), 1)).astype(bf16)
    position_c = as_column(position, HD)
    slot_c = as_column(slot, HD)
    which = (iota((RANKS, HD), 0) == offset).astype(bf16)
    named = jnp.where(position_c == (iota((HD, HD), 1) & 7), slot_c + 1, 0).astype(bf16)
    tab[...] = dot(which, named)

    pl.semaphore_wait(barrier, RANKS - 1)

    @pl.loop(1, RANKS)
    def _(k):
        pltpu.make_async_remote_copy(
            tab.at[pl.ds(k, 1)], tab_in.at[pl.ds(k, 1)], tab_send, tab_recv,
            device_id=ahead(k), device_id_type=MESH,
        ).start()

    tab_in[0:1] = tab[0:1]

    def slab(k):
        return pl.ds(pl.multiple_of(k * SLAB, SLAB), SLAB)

    for c in range(CHUNKS):
        cols = pl.ds(c * WIDTH, WIDTH)
        rows = jnp.concatenate([q_ref[:, cols], g_ref[:, cols]], axis=0)
        snd[c] = dot(pack[...], rows).astype(bf16)

        @pl.loop(1, RANKS)
        def _(k, c=c):
            pltpu.make_async_remote_copy(
                snd.at[c, slab(k)], rcv.at[c, slab(k)], in_send.at[c], in_recv.at[c],
                device_id=ahead(k), device_id_type=MESH,
            ).start()

        rcv[c, 0:SLAB] = snd[c, 0:SLAB]

    gk_t[...] = jnp.zeros_like(gk_t)
    gv_t[...] = jnp.zeros_like(gv_t)

    rest = pl.ds(1, RANKS - 1)
    pltpu.make_async_copy(tab.at[rest], tab_in.at[rest], tab_recv).wait()
    pltpu.make_async_copy(tab.at[rest], tab_in.at[rest], tab_send).wait()
    spread = jnp.broadcast_to(tab_in[...][:, None, :], (RANKS, SLAB, HD))
    pick = iota((RANKS, SLAB, HD), 2) == (iota((RANKS, SLAB, HD), 1) & 7)
    got = jnp.sum(jnp.where(pick, spread, 0.0), axis=2, keepdims=True)
    got = got.reshape(SLABS, 1).astype(jnp.int32) - 1
    is_far = [(owner_ref[image_ref[b]] != me).astype(jnp.int32) for b in range(4)]
    seat = jnp.full((SLABS, 1), -1, jnp.int32)
    half = (iota((SLABS, 1), 0) >> 3) & 1
    owns, fars = 0, 0
    for b in range(4):
        own_row = owns * 32 + half * OWN
        far_row = 2 * OWN + fars * 32 + half * FAR
        base = own_row + (far_row - own_row) * is_far[b]
        seat = jnp.where((got >> 5) == b, base + (got & 31), seat)
        fars = fars + is_far[b]
        owns = owns + 1 - is_far[b]
    unplace[...] = (seat == iota((SLABS, BAL), 1)).astype(bf16)
    seat_r = jnp.transpose(jnp.broadcast_to(seat, (SLABS, HD)))[:1]
    place[...] = (iota((BAL, SLABS), 0) == seat_r).astype(bf16)

    all_but_first = pl.ds(SLAB, SLABS - SLAB)
    far_rows = pl.ds(2 * OWN, 2 * FAR)

    def far_copy(c):
        return pltpu.make_async_remote_copy(
            bal.at[c, far_rows], far.at[c], far_send.at[c], far_recv.at[c],
            device_id=nxt, device_id_type=MESH,
        )

    def back_copy(c):
        return pltpu.make_async_remote_copy(
            back.at[c], res.at[c, far_rows], back_send.at[c], back_recv.at[c],
            device_id=prv, device_id_type=MESH,
        )

    def take_in(c):
        pltpu.make_async_copy(snd.at[c, all_but_first], rcv.at[c, all_but_first], in_recv.at[c]).wait()
        bal[c] = dot(place[...], rcv[c]).astype(bf16)
        far_copy(c).start()

    def send_out(c):
        back_copy(c).wait_recv()
        rep[c] = dot(unplace[...], res[c]).astype(bf16)

        @pl.loop(1, RANKS)
        def _(k):
            pltpu.make_async_remote_copy(
                rep.at[c, slab(k)], ret.at[c, slab(k)], out_send.at[c], out_recv.at[c],
                device_id=behind(k), device_id_type=MESH,
            ).start()

        ret[c, 0:SLAB] = rep[c, 0:SLAB]

    def gather_rows(c, own_at, far_at):
        parts = []
        for h in range(2):
            cols = slice(h * HD, (h + 1) * HD)
            parts += [bal[c, own_at : own_at + OWN, cols], far[c, far_at : far_at + FAR, cols]]
        return jnp.concatenate(parts, axis=0)

    def put_rows(c, x, own_at, far_at):
        for h in range(2):
            cols = slice(h * HD, (h + 1) * HD)
            top = h * (OWN + FAR)
            res[c, own_at : own_at + OWN, cols] = x[top : top + OWN]
            back[c, far_at : far_at + FAR, cols] = x[top + OWN : top + OWN + FAR]

    def keys_of(j):
        return pl.ds(pl.multiple_of(j * STEP, STEP), STEP)

    count = tiles_ref[0]
    take_in(0)

    @pl.loop(0, CHUNKS)
    def _(c):
        far_copy(c).wait_recv()
        q = gather_rows(c, 0, 0)
        g = gather_rows(c, OWN, FAR)

        def score_step(j, top):
            s = dot(q, k_ref[0, keys_of(j), :], NT)
            at = iota((1, STEP), 1) + j * STEP
            valid = (at % TOKP < TILE_TOK) & (at // TOKP < count)
            s = s + jnp.where(valid, 0.0, -1e30)
            scores[j] = s
            return jnp.maximum(top, fold(s, jnp.maximum))

        top = lax.fori_loop(0, STEPS, score_step, jnp.full((ROWS, HD), -3e38, f32))
        top = jnp.max(top, axis=1, keepdims=True) * (SCALE * LOG2E)

        def out_step(j, carry):
            total, out = carry
            e = jnp.exp2(scores[j] * (SCALE * LOG2E) - top)
            low = e.astype(bf16)
            weights[j] = low
            return total + fold(e, jnp.add), out + dot(low, v_ref[0, keys_of(j), :])

        zeros = jnp.zeros((ROWS, HD), f32)
        total, out = lax.fori_loop(0, STEPS, out_step, (zeros, zeros))
        inverse = 1.0 / jnp.sum(total, axis=1, keepdims=True)
        out = out * inverse
        put_rows(c, out.astype(bf16), 0, 0)

        @pl.when(c > 0)
        def _():
            send_out(c - 1)

        @pl.when(c < CHUNKS - 1)
        def _():
            take_in(c + 1)

        g32 = g.astype(f32)
        delta = jnp.sum(g32 * out, axis=1, keepdims=True)
        g_t = jnp.transpose(g32 * inverse).astype(bf16)
        q_t = jnp.transpose(q.astype(f32) * (inverse * SCALE)).astype(bf16)

        def grad_step(j, grad_q):
            dp = dot(g, v_ref[0, keys_of(j), :], NT)
            low = weights[j]
            ds = (low.astype(f32) * (dp - delta)).astype(bf16)
            gv_t[j] += dot(g_t, low)
            gk_t[j] += dot(q_t, ds)
            return grad_q + dot(ds, k_ref[0, keys_of(j), :])

        grad_q = lax.fori_loop(0, STEPS, grad_step, zeros)
        put_rows(c, (grad_q * (inverse * SCALE)).astype(bf16), OWN, FAR)
        back_copy(c).start()

    send_out(CHUNKS - 1)

    for j in range(STEPS):
        gk_ref[0, j * STEP : (j + 1) * STEP] = jnp.transpose(gk_t[j]).astype(bf16)
        gv_ref[0, j * STEP : (j + 1) * STEP] = jnp.transpose(gv_t[j]).astype(bf16)

    for c in range(CHUNKS):
        pltpu.make_async_copy(rep.at[c, all_but_first], ret.at[c, all_but_first], out_recv.at[c]).wait()
        final = dot(unpack[...], ret[c]).astype(bf16)
        cols = slice(c * WIDTH, (c + 1) * WIDTH)
        att_ref[:, cols] = final[:HD]
        gq_ref[:, cols] = final[HD:]

    for c in range(CHUNKS):
        pltpu.make_async_copy(snd.at[c, all_but_first], rcv.at[c, all_but_first], in_send.at[c]).wait()
        pltpu.make_async_copy(rep.at[c, all_but_first], ret.at[c, all_but_first], out_send.at[c]).wait()
        far_copy(c).wait_send()
        back_copy(c).wait_send()


def shards(queries, grad_out, row_dest, row_slot, block_image, image_owner, image_tiles, img_keys, img_values):
    vmem = pl.BlockSpec(memory_space=pltpu.VMEM)
    smem = pl.BlockSpec(memory_space=pltpu.SMEM)
    dma = pltpu.SemaphoreType.DMA
    slabs = pltpu.VMEM((CHUNKS, SLABS, WIDTH), bf16)
    return pl.pallas_call(
        kernel,
        out_shape=(
            jax.ShapeDtypeStruct(queries.shape, bf16),
            jax.ShapeDtypeStruct(queries.shape, bf16),
            jax.ShapeDtypeStruct(img_keys.shape, bf16),
            jax.ShapeDtypeStruct(img_keys.shape, bf16),
        ),
        in_specs=[smem] * 3 + [vmem] * 6,
        out_specs=(vmem,) * 4,
        scratch_shapes=[
            slabs, slabs, slabs, slabs,
            pltpu.VMEM((RANKS, HD), f32),
            pltpu.VMEM((RANKS, HD), f32),
            pltpu.VMEM((CHUNKS, BAL, WIDTH), bf16),
            pltpu.VMEM((CHUNKS, 2 * FAR, WIDTH), bf16),
            pltpu.VMEM((CHUNKS, BAL, WIDTH), bf16),
            pltpu.VMEM((CHUNKS, 2 * FAR, WIDTH), bf16),
            pltpu.VMEM((SLABS, 2 * HD), bf16),
            pltpu.VMEM((2 * HD, SLABS), bf16),
            pltpu.VMEM((BAL, SLABS), bf16),
            pltpu.VMEM((SLABS, BAL), bf16),
            pltpu.VMEM((STEPS, ROWS, STEP), f32),
            pltpu.VMEM((STEPS, ROWS, STEP), bf16),
            pltpu.VMEM((STEPS, HD, STEP), f32),
            pltpu.VMEM((STEPS, HD, STEP), f32),
            dma((CHUNKS,)), dma((CHUNKS,)), dma, dma,
            dma((CHUNKS,)), dma((CHUNKS,)), dma((CHUNKS,)), dma((CHUNKS,)),
            dma((CHUNKS,)), dma((CHUNKS,)),
        ],
        compiler_params=pltpu.CompilerParams(
            collective_id=0, has_side_effects=True, vmem_limit_bytes=56 * 1024 * 1024
        ),
    )(
        block_image, image_owner, image_tiles, row_dest.reshape(1, -1), row_slot.reshape(1, -1),
        queries, grad_out, img_keys, img_values,
    )


def solution(mesh):
    return jax.shard_map(
        shards,
        mesh=mesh,
        in_specs=(
            P("dp", "mp"),
            P("dp", "mp"),
            P("dp"),
            P("dp"),
            P("dp"),
            P(),
            P("dp"),
            P("dp", None, "mp"),
            P("dp", None, "mp"),
        ),
        out_specs=(P("dp", "mp"), P("dp", "mp"), P("dp", None, "mp"), P("dp", None, "mp")),
        check_vma=False,
    )
```

time: 508 us -> 107 us (0.21)
  waiting for transfers between devices: 224 us -> 0 us
  matrix products: 116 us -> 0 us
  Pallas kernels: 0 us -> 97.7 us
  local copies, waits for them, and re-layouts: 59.6 us -> 7.4 us
  other arithmetic: 46.2 us -> 0 us
  starting transfers between devices: 44.5 us -> 0 us
  loops' own time: 11.3 us -> 0 us
    all_to_all x3 -> x0, waiting for transfers between devices: 154 us -> none  [the longest x1 91.1 us: shards(): lax.all_to_all(reply.reshape(ranks, capacity, 2 * width), 'dp', split_axi...]
    dot_general x28 -> x0, matrix products: 116 us -> none  [the longest x4 34.6 us: head_pass(): lax.dot_general(probs_low, grad_rows, (((0,), (0,)), ((), ())), preferred...]
    pallas_call x0 -> x1, Pallas kernels: none -> 97.7 us  [shards(): pl.pallas_call(kernel, out_shape=(jax.ShapeDtypeStruct(queries.shape, bf1...]
    ppermute x5 -> x0, waiting for transfers between devices: 69.9 us -> none  [passed_along(): lax.ppermute(shard, axis, [(i, (i + by) % count) for i in range(count)])]
    all_to_all x3 -> x0, starting transfers between devices: 26.7 us -> none  [the longest x1 13.1 us: shards(): lax.all_to_all(reply.reshape(ranks, capacity, 2 * width), 'dp', split_axi...]
    dynamic_slice x20 -> x0, local copies, waits for them, and re-layouts: 22.2 us -> none  [the longest x8 10.4 us: visit_block(): source_rank = (image_owner[block_image[block_id]] - my_index) % ranks]
    ppermute x5 -> x0, starting transfers between devices: 17.7 us -> none  [passed_along(): lax.ppermute(shard, axis, [(i, (i + by) % count) for i in range(count)])]
    another operation x24 -> x0, local copies, waits for them, and re-layouts: 16.5 us -> none
  transfers between devices with their start and end apart: 8 -> 0, of which waited for: 4 -> 0; matrix products, arithmetic and copies ran while one was open for 5% -> 0% of each run, Pallas kernels for 0% -> 0%
where the time goes in v1:
time: 107 us; the launch traced here: 106 us
  Pallas kernels  97.7 us (91%)
  local copies, waits for them, and re-layouts  7.4 us (7%)
  between operations  1.29 us (1%)
    pallas_call x1, Pallas kernels, shards(): pl.pallas_call(kernel, out_shape=(jax.ShapeDtypeStruct(queries.shape, bf1...  97.7 us
    unnamed x6, local copies, waits for them, and re-layouts  7.4 us

profile of v1, /device:TPU:8, one launch (start us, length us, event | category | flops | bytes accessed | tf_op | source)
XLA Modules:
  0.0 106.4 jit_solution(11239133618625274560)
XLA Ops:
  1.3 97.7 %shard_map.120 = (bf16[128,1024]{1,0:T(8,128)(2,1)}, bf16[128,1024]{1,0:T(8,128)(2,1)}, bf16[1,6656,128]{2,1,0:T(8,128)(2,1)}, bf16[1,6656,128]{2,1,0:T(8,128)(2,1)}) custom-call(s32[4]{0:T(128)} %image_ref.1, s32[32]{0:T(128)} %owner_ref.1, s32[1]{0:T(128)S(6)} %copy.17.tiles_ref, s32[1,128]{1,0:T(1,128)} %bitcast.2, s32[1,128]{1,0:T(1,128)} %bitcast.3, ...), custom_call_target="tpu_custom_call" | custom-call | tf_op jit(solution)/shard_map/pallas_call | solution.py:278
  99.0 1.7 %copy.18 = bf16[128,1024]{1,0:T(8,128)(2,1)} copy(bf16[128,1024]{1,0:T(8,128)(2,1)} %get-tuple-element.8) | data formatting | bytes 524288
  100.6 1.7 %copy.19 = bf16[128,1024]{1,0:T(8,128)(2,1)} copy(bf16[128,1024]{1,0:T(8,128)(2,1)} %get-tuple-element.9) | data formatting | bytes 524288
  102.3 0.0 copy-start
  102.3 2.9 %copy.20 = bf16[1,6656,128]{2,1,0:T(8,128)(2,1)} copy(bf16[1,6656,128]{2,1,0:T(8,128)(2,1)} %get-tuple-element.10) | data formatting | bytes 3407872
  105.2 0.0 copy-done
  105.2 1.2 %copy.21 = bf16[1,6656,128]{2,1,0:T(8,128)(2,1)} copy(bf16[1,6656,128]{2,1,0:T(8,128)(2,1)S(1)} %copy-done) | data formatting | bytes 3407872
Async XLA Ops:
  102.3 2.9 %copy-start = (bf16[1,6656,128]{2,1,0:T(8,128)(2,1)S(1)}, bf16[1,6656,128]{2,1,0:T(8,128)(2,1)}, u32[]{:S(2)}) copy-start(bf16[1,6656,128]{2,1,0:T(8,128)(2,1)} %get-tuple-element.11) | copy-start | bytes 5111812

commit v2 on v1

--- a/solution.py
+++ b/solution.py
@@ -24,6 +24,8 @@
 ROWS = 2 * (OWN + FAR)
 STEP = 3328
 STEPS = KEYS // STEP
+AHEAD = 2
+PARTS = 4
 MESH = pl.DeviceIdType.MESH
 f32 = jnp.float32
 bf16 = jnp.bfloat16
@@ -54,8 +56,8 @@
     image_ref, owner_ref, tiles_ref, dest_ref, slot_ref, q_ref, g_ref, k_ref, v_ref,
     att_ref, gq_ref, gk_ref, gv_ref,
     snd, rcv, rep, ret, tab, tab_in, bal, far, res, back,
-    pack, unpack, place, unplace, scores, weights, gk_t, gv_t,
-    in_send, in_recv, tab_send, tab_recv, far_send, far_recv, back_send, back_recv, out_send, out_recv,
+    pack, unpack, place, unplace, scores, weights, slopes, q_low, g_low, k_buf, v_buf,
+    held, in_send, in_recv, tab_send, tab_recv, far_send, far_recv, back_send, back_recv, out_send, out_recv,
 ):
     me = lax.axis_index("dp")
     mz, mx = me // 4, me % 4
@@ -69,6 +71,12 @@
     nxt = {"dp": (me + 1) % RANKS}
     prv = {"dp": (me + RANKS - 1) % RANKS}
     barrier = pltpu.get_barrier_semaphore()
+    get_k = pltpu.make_async_copy(k_ref.at[0], k_buf, held.at[0])
+    get_v = pltpu.make_async_copy(v_ref.at[0], v_buf, held.at[1])
+    put_k = pltpu.make_async_copy(k_buf, gk_ref.at[0], held.at[0])
+    put_v = pltpu.make_async_copy(v_buf, gv_ref.at[0], held.at[1])
+    get_k.start()
+    get_v.start()
 
     @pl.loop(1, RANKS)
     def _(k):
@@ -89,6 +97,13 @@
     named = jnp.where(position_c == (iota((HD, HD), 1) & 7), slot_c + 1, 0).astype(bf16)
     tab[...] = dot(which, named)
 
+    for c in range(CHUNKS):
+        cols = slice(c * WIDTH, (c + 1) * WIDTH)
+        rows = jnp.concatenate([q_ref[:, cols], g_ref[:, cols]], axis=0)
+        snd[c] = dot(pack[...], rows).astype(bf16)
+        rcv[c, 0:SLAB] = snd[c, 0:SLAB]
+    tab_in[0:1] = tab[0:1]
+
     pl.semaphore_wait(barrier, RANKS - 1)
 
     @pl.loop(1, RANKS)
@@ -98,27 +113,19 @@
             device_id=ahead(k), device_id_type=MESH,
         ).start()
 
-    tab_in[0:1] = tab[0:1]
-
     def slab(k):
         return pl.ds(pl.multiple_of(k * SLAB, SLAB), SLAB)
 
-    for c in range(CHUNKS):
-        cols = pl.ds(c * WIDTH, WIDTH)
-        rows = jnp.concatenate([q_ref[:, cols], g_ref[:, cols]], axis=0)
-        snd[c] = dot(pack[...], rows).astype(bf16)
-
+    def send_in(c):
         @pl.loop(1, RANKS)
-        def _(k, c=c):
+        def _(k):
             pltpu.make_async_remote_copy(
                 snd.at[c, slab(k)], rcv.at[c, slab(k)], in_send.at[c], in_recv.at[c],
                 device_id=ahead(k), device_id_type=MESH,
             ).start()
 
-        rcv[c, 0:SLAB] = snd[c, 0:SLAB]
-
-    gk_t[...] = jnp.zeros_like(gk_t)
-    gv_t[...] = jnp.zeros_like(gv_t)
+    for c in range(AHEAD):
+        send_in(c)
 
     rest = pl.ds(1, RANKS - 1)
     pltpu.make_async_copy(tab.at[rest], tab_in.at[rest], tab_recv).wait()
@@ -159,8 +166,14 @@
 
     def take_in(c):
         pltpu.make_async_copy(snd.at[c, all_but_first], rcv.at[c, all_but_first], in_recv.at[c]).wait()
-        bal[c] = dot(place[...], rcv[c]).astype(bf16)
+        bal[c, 2 * OWN :] = dot(place[2 * OWN :], rcv[c]).astype(bf16)
         far_copy(c).start()
+
+        @pl.when(c + AHEAD < CHUNKS)
+        def _():
+            send_in(c + AHEAD)
+
+        bal[c, : 2 * OWN] = dot(place[: 2 * OWN], rcv[c]).astype(bf16)
 
     def send_out(c):
         back_copy(c).wait_recv()
@@ -194,15 +207,18 @@
 
     count = tiles_ref[0]
     take_in(0)
+    get_k.wait()
+    get_v.wait()
 
     @pl.loop(0, CHUNKS)
     def _(c):
+        pairs = pl.ds(pl.multiple_of(c * ROWS, ROWS), ROWS)
         far_copy(c).wait_recv()
         q = gather_rows(c, 0, 0)
         g = gather_rows(c, OWN, FAR)
 
         def score_step(j, top):
-            s = dot(q, k_ref[0, keys_of(j), :], NT)
+            s = dot(q, k_buf[keys_of(j), :], NT)
             at = iota((1, STEP), 1) + j * STEP
             valid = (at % TOKP < TILE_TOK) & (at // TOKP < count)
             s = s + jnp.where(valid, 0.0, -1e30)
@@ -212,12 +228,16 @@
         top = lax.fori_loop(0, STEPS, score_step, jnp.full((ROWS, HD), -3e38, f32))
         top = jnp.max(top, axis=1, keepdims=True) * (SCALE * LOG2E)
 
+        @pl.when(c < CHUNKS - 1)
+        def _():
+            take_in(c + 1)
+
         def out_step(j, carry):
             total, out = carry
             e = jnp.exp2(scores[j] * (SCALE * LOG2E) - top)
             low = e.astype(bf16)
-            weights[j] = low
-            return total + fold(e, jnp.add), out + dot(low, v_ref[0, keys_of(j), :])
+            weights[j, pairs] = low
+            return total + fold(e, jnp.add), out + dot(low, v_buf[keys_of(j), :])
 
         zeros = jnp.zeros((ROWS, HD), f32)
         total, out = lax.fori_loop(0, STEPS, out_step, (zeros, zeros))
@@ -225,36 +245,36 @@
         out = out * inverse
         put_rows(c, out.astype(bf16), 0, 0)
 
+        g32 = g.astype(f32)
+        delta = jnp.sum(g32 * out, axis=1, keepdims=True)
+        g_low[pairs] = (g32 * inverse).astype(bf16)
+        q_low[pairs] = (q.astype(f32) * (inverse * SCALE)).astype(bf16)
+
+        def grad_step(j, grad_q):
+            dp = dot(g, v_buf[keys_of(j), :], NT)
+            ds = (weights[j, pairs].astype(f32) * (dp - delta)).astype(bf16)
+            slopes[j, pairs] = ds
+            return grad_q + dot(ds, k_buf[keys_of(j), :])
+
+        grad_q = lax.fori_loop(0, STEPS, grad_step, zeros)
+        put_rows(c, (grad_q * (inverse * SCALE)).astype(bf16), OWN, FAR)
+        back_copy(c).start()
+
         @pl.when(c > 0)
         def _():
             send_out(c - 1)
 
-        @pl.when(c < CHUNKS - 1)
-        def _():
-            take_in(c + 1)
-
-        g32 = g.astype(f32)
-        delta = jnp.sum(g32 * out, axis=1, keepdims=True)
-        g_t = jnp.transpose(g32 * inverse).astype(bf16)
-        q_t = jnp.transpose(q.astype(f32) * (inverse * SCALE)).astype(bf16)
-
-        def grad_step(j, grad_q):
-            dp = dot(g, v_ref[0, keys_of(j), :], NT)
-            low = weights[j]
-            ds = (low.astype(f32) * (dp - delta)).astype(bf16)
-            gv_t[j] += dot(g_t, low)
-            gk_t[j] += dot(q_t, ds)
-            return grad_q + dot(ds, k_ref[0, keys_of(j), :])
-
-        grad_q = lax.fori_loop(0, STEPS, grad_step, zeros)
-        put_rows(c, (grad_q * (inverse * SCALE)).astype(bf16), OWN, FAR)
-        back_copy(c).start()
-
+    g_t = jnp.transpose(g_low[...].astype(f32)).astype(bf16)
+    q_t = jnp.transpose(q_low[...].astype(f32)).astype(bf16)
+    k_buf[0:STEP] = jnp.transpose(dot(q_t, slopes[0])).astype(bf16)
     send_out(CHUNKS - 1)
-
     for j in range(STEPS):
-        gk_ref[0, j * STEP : (j + 1) * STEP] = jnp.transpose(gk_t[j]).astype(bf16)
-        gv_ref[0, j * STEP : (j + 1) * STEP] = jnp.transpose(gv_t[j]).astype(bf16)
+        mine = slice(j * STEP, (j + 1) * STEP)
+        v_buf[mine] = jnp.transpose(dot(g_t, weights[j])).astype(bf16)
+        if j:
+            k_buf[mine] = jnp.transpose(dot(q_t, slopes[j])).astype(bf16)
+    put_k.start()
+    put_v.start()
 
     for c in range(CHUNKS):
         pltpu.make_async_copy(rep.at[c, all_but_first], ret.at[c, all_but_first], out_recv.at[c]).wait()
@@ -268,23 +288,43 @@
         pltpu.make_async_copy(rep.at[c, all_but_first], ret.at[c, all_but_first], out_send.at[c]).wait()
         far_copy(c).wait_send()
         back_copy(c).wait_send()
+    put_k.wait()
+    put_v.wait()
+
+
+def finish(*refs):
+    sems = refs[-1]
+    moves = []
+    for a, (src, dst, via) in enumerate(zip(refs[:4], refs[4:8], refs[8:12])):
+        axis = src.shape.index(max(src.shape))
+        part = src.shape[axis] // PARTS
+        for p in range(PARTS):
+            at = (slice(None),) * axis + (pl.ds(p * part, part),)
+            moves.append((
+                pltpu.make_async_copy(src.at[at], via.at[at], sems.at[0, a, p]),
+                pltpu.make_async_copy(via.at[at], dst.at[at], sems.at[1, a, p]),
+            ))
+    for come, _ in moves:
+        come.start()
+    for come, go in moves:
+        come.wait()
+        go.start()
+    for _, go in moves:
+        go.wait()
 
 
 def shards(queries, grad_out, row_dest, row_slot, block_image, image_owner, image_tiles, img_keys, img_values):
     vmem = pl.BlockSpec(memory_space=pltpu.VMEM)
     smem = pl.BlockSpec(memory_space=pltpu.SMEM)
+    hbm = pl.BlockSpec(memory_space=pl.ANY)
     dma = pltpu.SemaphoreType.DMA
     slabs = pltpu.VMEM((CHUNKS, SLABS, WIDTH), bf16)
-    return pl.pallas_call(
+    shapes = tuple(jax.ShapeDtypeStruct(x.shape, bf16) for x in (queries, grad_out, img_keys, img_values))
+    results = pl.pallas_call(
         kernel,
-        out_shape=(
-            jax.ShapeDtypeStruct(queries.shape, bf16),
-            jax.ShapeDtypeStruct(queries.shape, bf16),
-            jax.ShapeDtypeStruct(img_keys.shape, bf16),
-            jax.ShapeDtypeStruct(img_keys.shape, bf16),
-        ),
-        in_specs=[smem] * 3 + [vmem] * 6,
-        out_specs=(vmem,) * 4,
+        out_shape=shapes,
+        in_specs=[smem] * 3 + [vmem] * 4 + [hbm] * 2,
+        out_specs=(vmem, vmem, hbm, hbm),
         scratch_shapes=[
             slabs, slabs, slabs, slabs,
             pltpu.VMEM((RANKS, HD), f32),
@@ -298,20 +338,32 @@
             pltpu.VMEM((BAL, SLABS), bf16),
             pltpu.VMEM((SLABS, BAL), bf16),
             pltpu.VMEM((STEPS, ROWS, STEP), f32),
-            pltpu.VMEM((STEPS, ROWS, STEP), bf16),
-            pltpu.VMEM((STEPS, HD, STEP), f32),
-            pltpu.VMEM((STEPS, HD, STEP), f32),
+            pltpu.VMEM((STEPS, CHUNKS * ROWS, STEP), bf16),
+            pltpu.VMEM((STEPS, CHUNKS * ROWS, STEP), bf16),
+            pltpu.VMEM((CHUNKS * ROWS, HD), bf16),
+            pltpu.VMEM((CHUNKS * ROWS, HD), bf16),
+            pltpu.VMEM((KEYS, HD), bf16),
+            pltpu.VMEM((KEYS, HD), bf16),
+            dma((2,)),
             dma((CHUNKS,)), dma((CHUNKS,)), dma, dma,
             dma((CHUNKS,)), dma((CHUNKS,)), dma((CHUNKS,)), dma((CHUNKS,)),
             dma((CHUNKS,)), dma((CHUNKS,)),
         ],
         compiler_params=pltpu.CompilerParams(
-            collective_id=0, has_side_effects=True, vmem_limit_bytes=56 * 1024 * 1024
+            collective_id=0, has_side_effects=True, vmem_limit_bytes=62 * 1024 * 1024
         ),
     )(
         block_image, image_owner, image_tiles, row_dest.reshape(1, -1), row_slot.reshape(1, -1),
         queries, grad_out, img_keys, img_values,
     )
+    return pl.pallas_call(
+        finish,
+        out_shape=shapes,
+        in_specs=[hbm] * 4,
+        out_specs=(hbm,) * 4,
+        scratch_shapes=[pltpu.VMEM(x.shape, bf16) for x in shapes] + [dma((2, 4, PARTS))],
+        compiler_params=pltpu.CompilerParams(vmem_limit_bytes=62 * 1024 * 1024),
+    )(*results)
 
 
 def solution(mesh):

time: 107 us -> 80 us (0.75)
  Pallas kernels: 97.7 us -> 78.6 us
  local copies, waits for them, and re-layouts: 7.4 us -> 0 us
    pallas_call x1 -> x2, Pallas kernels: 97.7 us -> 78.6 us  [the longest x1 74.8 us: shards(): pl.pallas_call(kernel, out_shape=shapes, in_specs=[smem] * 3 + [vmem] * 4...]
    unnamed x6 -> x0, local copies, waits for them, and re-layouts: 7.4 us -> none
where the time goes in v2:
time: 80 us; the launch traced here: 79.9 us
  Pallas kernels  78.6 us (98%)
  between operations  1.29 us (2%)
    pallas_call x1, Pallas kernels, shards(): pl.pallas_call(kernel, out_shape=shapes, in_specs=[smem] * 3 + [vmem] * 4...  74.8 us
    pallas_call x1, Pallas kernels, shards(): pl.pallas_call(finish, out_shape=shapes, in_specs=[hbm] * 4, out_specs=(h...  3.84 us

profile of v2, /device:TPU:8, one launch (start us, length us, event | category | flops | bytes accessed | tf_op | source)
XLA Modules:
  0.0 79.9 jit_solution(17921929538751829942)
XLA Ops:
  1.3 74.8 %shard_map.120 = (bf16[128,1024]{1,0:T(8,128)(2,1)}, bf16[128,1024]{1,0:T(8,128)(2,1)}, bf16[1,6656,128]{2,1,0:T(8,128)(2,1)}, bf16[1,6656,128]{2,1,0:T(8,128)(2,1)}) custom-call(s32[4]{0:T(128)} %image_ref.1, s32[32]{0:T(128)} %owner_ref.1, s32[1]{0:T(128)S(6)} %copy.13.tiles_ref, s32[1,128]{1,0:T(1,128)} %bitcast.2, s32[1,128]{1,0:T(1,128)} %bitcast.3, ...), custom_call_target="tpu_custom_call" | custom-call | tf_op jit(solution)/shard_map/pallas_call | solution.py:323
  76.1 3.8 %shard_map.121 = (bf16[128,1024]{1,0:T(8,128)(2,1)}, bf16[128,1024]{1,0:T(8,128)(2,1)}, bf16[1,6656,128]{2,1,0:T(8,128)(2,1)}, bf16[1,6656,128]{2,1,0:T(8,128)(2,1)}) custom-call(bf16[128,1024]{1,0:T(8,128)(2,1)} %get-tuple-element.8.refs_0_, bf16[128,1024]{1,0:T(8,128)(2,1)} %get-tuple-element.9.refs_1_, bf16[1,6656,128]{2,1,0:T(8,128)(2,1)} %get-tuple-element.10.refs_2_, ...), custom_call_target="tpu_custom_call" | custom-call | tf_op jit(solution)/shard_map/pallas_call | solution.py:359

commit v3 on v2

v3 whole, which is shorter than its diff:
```python
import functools

import jax
import jax.numpy as jnp
from jax import lax
from jax.experimental import pallas as pl
from jax.experimental.pallas import tpu as pltpu
from jax.sharding import PartitionSpec as P

HD = 128
TILE_TOK = 1601
TOKP = 1664
KEYS = 6656
SCALE = HD**-0.5
LOG2E = 1.4426950408889634
RANKS = 32
CHUNKS = 4
WIDTH = 256
SLAB = 16
SLABS = RANKS * SLAB
OWN = 96
FAR = 64
BAL = 2 * (OWN + FAR)
ROWS = 2 * (OWN + FAR)
STEP = 3328
STEPS = KEYS // STEP
AHEAD = 2
MESH = pl.DeviceIdType.MESH
f32 = jnp.float32
bf16 = jnp.bfloat16
NT = ((1,), (1,))
NN = ((1,), (0,))


def dot(a, b, dims=NN):
    return lax.dot_general(a, b, (dims, ((), ())), preferred_element_type=f32)


def iota(shape, dim):
    return lax.broadcasted_iota(jnp.int32, shape, dim)


def fold(x, op):
    r = x[:, :HD]
    for i in range(1, x.shape[1] // HD):
        r = op(r, x[:, i * HD : (i + 1) * HD])
    return r


def as_column(row, n):
    return jnp.transpose(jnp.broadcast_to(row, (HD, n)))[:, :1]


def kernel(
    image_ref, owner_ref, tiles_ref, dest_ref, slot_ref, q_ref, g_ref, k_ref, v_ref,
    att_ref, gq_ref, k_buf, v_buf,
    snd, rcv, rep, ret, tab, tab_in, bal, far, res, back,
    pack, unpack, place, unplace, scores, weights, slopes, q_low, g_low, rows,
    entered, held, in_send, in_recv, tab_send, tab_recv, far_send, far_recv, back_send, back_recv, out_send, out_recv,
):
    me = lax.axis_index("dp")
    mz, mx = me >> 2, me & 3

    def ahead(k):
        return {"dp": ((mz + (k >> 2)) & 7) * 4 + ((mx + (k & 3)) & 3)}

    def behind(k):
        return {"dp": ((mz + 8 - (k >> 2)) & 7) * 4 + ((mx + 4 - (k & 3)) & 3)}

    def to_all(send):
        for k in range(1, 4):
            send(k)

        @pl.loop(1, 8)
        def _(dz):
            for dx in range(4):
                send(dz * 4 + dx)

    nxt = {"dp": (me + 1) & (RANKS - 1)}
    prv = {"dp": (me + RANKS - 1) & (RANKS - 1)}
    barrier = pltpu.get_barrier_semaphore()
    get_k = pltpu.make_async_copy(k_ref, k_buf, held.at[0])
    get_v = pltpu.make_async_copy(v_ref, v_buf, held.at[1])
    get_q = pltpu.make_async_copy(q_ref, rows.at[pl.ds(0, HD)], held.at[2])
    get_g = pltpu.make_async_copy(g_ref, rows.at[pl.ds(HD, HD)], held.at[3])
    get_q.start()
    get_g.start()
    get_k.start()
    get_v.start()

    lines = [k for k in range(1, RANKS) if k < 4 or k % 4 == 0]
    for k in lines:
        pl.semaphore_signal(barrier, 1, device_id=ahead(k), device_id_type=MESH)

    dest = dest_ref[...]
    slot = slot_ref[...]
    offset = (((dest >> 2) - mz) & 7) * 4 + (((dest & 3) - mx) & 3)
    dest_c = as_column(dest, HD)
    same = (dest_c == dest) & (iota((HD, HD), 0) < iota((HD, HD), 1))
    position = jnp.sum(same.astype(jnp.int32), axis=0, keepdims=True)
    target = jnp.concatenate([offset * SLAB + position, offset * SLAB + 8 + position], axis=1)
    pack[...] = (iota((SLABS, 2 * HD), 0) == target).astype(bf16)
    position_c = as_column(position, HD)
    slot_c = as_column(slot, HD)
    which = (iota((RANKS, HD), 0) == offset).astype(bf16)
    named = jnp.where(position_c == (iota((HD, HD), 1) & 7), slot_c + 1, 0).astype(bf16)
    tab[...] = dot(which, named)

    def fill(c):
        cols = slice(c * WIDTH, (c + 1) * WIDTH)
        snd[c] = dot(pack[...], rows[:, cols]).astype(bf16)
        rcv[c, 0:SLAB] = snd[c, 0:SLAB]

    get_q.wait()
    get_g.wait()
    fill(0)
    tab_in[0:1] = tab[0:1]
    pl.semaphore_wait(barrier, len(lines))
    for k in range(1, 4):
        pl.semaphore_signal(entered, 1, device_id=ahead(k), device_id_type=MESH)
    pl.semaphore_wait(entered, 3)

    def slab(k):
        return pl.ds(k * SLAB if isinstance(k, int) else pl.multiple_of(k * SLAB, SLAB), SLAB)

    def send_in(c):
        def one(k):
            pltpu.make_async_remote_copy(
                snd.at[c, slab(k)], rcv.at[c, slab(k)], in_send.at[c], in_recv.at[c],
                device_id=ahead(k), device_id_type=MESH,
            ).start()

        to_all(one)

    send_in(0)
    def one(k):
        pltpu.make_async_remote_copy(
            tab.at[pl.ds(k, 1)], tab_in.at[pl.ds(k, 1)], tab_send, tab_recv,
            device_id=ahead(k), device_id_type=MESH,
        ).start()

    to_all(one)
    for c in range(1, AHEAD):
        fill(c)
        send_in(c)
    for c in range(AHEAD, CHUNKS):
        fill(c)
    unpack[...] = (as_column(target, 2 * HD) == iota((2 * HD, SLABS), 1)).astype(bf16)

    rest = pl.ds(1, RANKS - 1)
    pltpu.make_async_copy(tab.at[rest], tab_in.at[rest], tab_recv).wait()
    pltpu.make_async_copy(tab.at[rest], tab_in.at[rest], tab_send).wait()
    spread = jnp.broadcast_to(tab_in[...][:, None, :], (RANKS, SLAB, HD))
    pick = iota((RANKS, SLAB, HD), 2) == (iota((RANKS, SLAB, HD), 1) & 7)
    got = jnp.sum(jnp.where(pick, spread, 0.0), axis=2, keepdims=True)
    got = got.reshape(SLABS, 1).astype(jnp.int32) - 1
    is_far = [(owner_ref[image_ref[b]] != me).astype(jnp.int32) for b in range(4)]
    seat = jnp.full((SLABS, 1), -1, jnp.int32)
    half = (iota((SLABS, 1), 0) >> 3) & 1
    owns, fars = 0, 0
    for b in range(4):
        own_row = owns * 32 + half * OWN
        far_row = 2 * OWN + fars * 32 + half * FAR
        base = own_row + (far_row - own_row) * is_far[b]
        seat = jnp.where((got >> 5) == b, base + (got & 31), seat)
        fars = fars + is_far[b]
        owns = owns + 1 - is_far[b]
    unplace[...] = (seat == iota((SLABS, BAL), 1)).astype(bf16)
    seat_r = jnp.transpose(jnp.broadcast_to(seat, (SLABS, HD)))[:1]
    place[...] = (iota((BAL, SLABS), 0) == seat_r).astype(bf16)

    all_but_first = pl.ds(SLAB, SLABS - SLAB)
    far_rows = pl.ds(2 * OWN, 2 * FAR)

    def far_copy(c):
        return pltpu.make_async_remote_copy(
            bal.at[c, far_rows], far.at[c], far_send.at[c], far_recv.at[c],
            device_id=nxt, device_id_type=MESH,
        )

    def back_copy(c):
        return pltpu.make_async_remote_copy(
            back.at[c], res.at[c, far_rows], back_send.at[c], back_recv.at[c],
            device_id=prv, device_id_type=MESH,
        )

    def take_in(c):
        pltpu.make_async_copy(snd.at[c, all_but_first], rcv.at[c, all_but_first], in_recv.at[c]).wait()
        bal[c, 2 * OWN :] = dot(place[2 * OWN :], rcv[c]).astype(bf16)
        far_copy(c).start()

        if isinstance(c, int):
            if c + AHEAD < CHUNKS:
                send_in(c + AHEAD)
        else:

            @pl.when(c + AHEAD < CHUNKS)
            def _():
                send_in(c + AHEAD)

        bal[c, : 2 * OWN] = dot(place[: 2 * OWN], rcv[c]).astype(bf16)

    def send_out(c):
        back_copy(c).wait_recv()
        rep[c] = dot(unplace[...], res[c]).astype(bf16)

        def one(k):
            pltpu.make_async_remote_copy(
                rep.at[c, slab(k)], ret.at[c, slab(k)], out_send.at[c], out_recv.at[c],
                device_id=behind(k), device_id_type=MESH,
            ).start()

        to_all(one)

        ret[c, 0:SLAB] = rep[c, 0:SLAB]

    def segments(group):
        own = [(bal, res, 0, OWN, OWN, h) for h in range(2)]
        away = [(far, back, 0, FAR, FAR, h) for h in range(2)]
        return {"own": own, "far": away, "all": own + away}[group]

    def gather_rows(c, group, second):
        parts = []
        for src, _, first, other, n, h in segments(group):
            at = other if second else first
            parts.append(src[c, at : at + n, h * HD : (h + 1) * HD])
        return jnp.concatenate(parts, axis=0)

    def put_rows(c, group, second, x):
        top = 0
        for _, dst, first, other, n, h in segments(group):
            at = other if second else first
            dst[c, at : at + n, h * HD : (h + 1) * HD] = x[top : top + n]
            top += n

    def keys_of(j):
        return pl.ds(pl.multiple_of(j * STEP, STEP), STEP)

    count = tiles_ref[0]
    take_in(0)
    get_k.wait()
    get_v.wait()

    def attend(c, group, between=None):
        low_at = 2 * OWN if group == "far" else 0
        n = {"own": 2 * OWN, "far": 2 * FAR, "all": ROWS}[group]
        pairs = pl.ds(pl.multiple_of(c * ROWS + low_at, 64), n)
        q = gather_rows(c, group, False)
        g = gather_rows(c, group, True)

        def score_step(j, top):
            s = dot(q, k_buf[0, keys_of(j), :], NT)
            at = iota((1, STEP), 1) + j * STEP
            valid = (at % TOKP < TILE_TOK) & (at // TOKP < count)
            s = s + jnp.where(valid, 0.0, -1e30)
            scores[j, :n] = s
            return jnp.maximum(top, fold(s, jnp.maximum))

        top = lax.fori_loop(0, STEPS, score_step, jnp.full((n, HD), -3e38, f32))
        top = jnp.max(top, axis=1, keepdims=True) * (SCALE * LOG2E)
        if between is not None:
            between()

        def out_step(j, carry):
            total, out = carry
            e = jnp.exp2(scores[j, :n] * (SCALE * LOG2E) - top)
            low = e.astype(bf16)
            weights[j, pairs] = low
            return total + fold(e, jnp.add), out + dot(low, v_buf[0, keys_of(j), :])

        zeros = jnp.zeros((n, HD), f32)
        total, out = lax.fori_loop(0, STEPS, out_step, (zeros, zeros))
        inverse = 1.0 / jnp.sum(total, axis=1, keepdims=True)
        out = out * inverse
        put_rows(c, group, False, out.astype(bf16))
        g32 = g.astype(f32)
        delta = jnp.sum(g32 * out, axis=1, keepdims=True)
        g_low[pairs] = (g32 * inverse).astype(bf16)
        q_low[pairs] = (q.astype(f32) * (inverse * SCALE)).astype(bf16)

        def grad_step(j, grad_q):
            dp = dot(g, v_buf[0, keys_of(j), :], NT)
            ds = (weights[j, pairs].astype(f32) * (dp - delta)).astype(bf16)
            slopes[j, pairs] = ds
            return grad_q + dot(ds, k_buf[0, keys_of(j), :])

        grad_q = lax.fori_loop(0, STEPS, grad_step, zeros)
        put_rows(c, group, True, (grad_q * (inverse * SCALE)).astype(bf16))

    attend(0, "own")
    far_copy(0).wait_recv()
    attend(0, "far", lambda: take_in(1))
    back_copy(0).start()

    @pl.loop(1, CHUNKS)
    def _(c):
        far_copy(c).wait_recv()

        def between():
            @pl.when(c < CHUNKS - 1)
            def _():
                take_in(c + 1)

        attend(c, "all", between)
        back_copy(c).start()
        send_out(c - 1)

    g_t = jnp.transpose(g_low[...].astype(f32)).astype(bf16)
    q_t = jnp.transpose(q_low[...].astype(f32)).astype(bf16)
    for j in range(STEPS):
        mine = slice(j * STEP, (j + 1) * STEP)
        k_buf[0, mine] = jnp.transpose(dot(q_t, slopes[j])).astype(bf16)
        v_buf[0, mine] = jnp.transpose(dot(g_t, weights[j])).astype(bf16)
        if j == 0:
            send_out(CHUNKS - 1)

    for c in range(CHUNKS):
        pltpu.make_async_copy(rep.at[c, all_but_first], ret.at[c, all_but_first], out_recv.at[c]).wait()
        final = dot(unpack[...], ret[c]).astype(bf16)
        cols = slice(c * WIDTH, (c + 1) * WIDTH)
        att_ref[:, cols] = final[:HD]
        gq_ref[:, cols] = final[HD:]

    for c in range(CHUNKS):
        pltpu.make_async_copy(snd.at[c, all_but_first], rcv.at[c, all_but_first], in_send.at[c]).wait()
        pltpu.make_async_copy(rep.at[c, all_but_first], ret.at[c, all_but_first], out_send.at[c]).wait()
        far_copy(c).wait_send()
        back_copy(c).wait_send()


def finish(*refs):
    copies = [
        pltpu.make_async_copy(src, dst, refs[-1].at[i])
        for i, (src, dst) in enumerate(zip(refs[:4], refs[4:8]))
    ]
    for copy in copies:
        copy.start()
    for copy in copies:
        copy.wait()


def shards(queries, grad_out, row_dest, row_slot, block_image, image_owner, image_tiles, img_keys, img_values):
    vmem = pl.BlockSpec(memory_space=pltpu.VMEM)
    smem = pl.BlockSpec(memory_space=pltpu.SMEM)
    hbm = pl.BlockSpec(memory_space=pl.ANY)
    dma = pltpu.SemaphoreType.DMA
    slabs = pltpu.VMEM((CHUNKS, SLABS, WIDTH), bf16)
    shapes = tuple(jax.ShapeDtypeStruct(x.shape, bf16) for x in (queries, grad_out, img_keys, img_values))
    results = pl.pallas_call(
        kernel,
        out_shape=tuple(pltpu.VMEM(x.shape, bf16) for x in shapes),
        in_specs=[smem] * 3 + [vmem] * 2 + [hbm] * 4,
        out_specs=(vmem,) * 4,
        scratch_shapes=[
            slabs, slabs, slabs, slabs,
            pltpu.VMEM((RANKS, HD), f32),
            pltpu.VMEM((RANKS, HD), f32),
            pltpu.VMEM((CHUNKS, BAL, WIDTH), bf16),
            pltpu.VMEM((CHUNKS, 2 * FAR, WIDTH), bf16),
            pltpu.VMEM((CHUNKS, BAL, WIDTH), bf16),
            pltpu.VMEM((CHUNKS, 2 * FAR, WIDTH), bf16),
            pltpu.VMEM((SLABS, 2 * HD), bf16),
            pltpu.VMEM((2 * HD, SLABS), bf16),
            pltpu.VMEM((BAL, SLABS), bf16),
            pltpu.VMEM((SLABS, BAL), bf16),
            pltpu.VMEM((STEPS, ROWS, STEP), f32),
            pltpu.VMEM((STEPS, CHUNKS * ROWS, STEP), bf16),
            pltpu.VMEM((STEPS, CHUNKS * ROWS, STEP), bf16),
            pltpu.VMEM((CHUNKS * ROWS, HD), bf16),
            pltpu.VMEM((CHUNKS * ROWS, HD), bf16),
            pltpu.VMEM((2 * HD, queries.shape[1]), bf16),
            pltpu.SemaphoreType.REGULAR,
            dma((4,)),
            dma((CHUNKS,)), dma((CHUNKS,)), dma, dma,
            dma((CHUNKS,)), dma((CHUNKS,)), dma((CHUNKS,)), dma((CHUNKS,)),
            dma((CHUNKS,)), dma((CHUNKS,)),
        ],
        compiler_params=pltpu.CompilerParams(
            collective_id=0, has_side_effects=True, vmem_limit_bytes=59 * 1024 * 1024
        ),
    )(
        block_image, image_owner, image_tiles, row_dest.reshape(1, -1), row_slot.reshape(1, -1),
        queries, grad_out, img_keys, img_values,
    )
    return pl.pallas_call(
        finish,
        out_shape=shapes,
        in_specs=[hbm] * 4,
        out_specs=(hbm,) * 4,
        scratch_shapes=[dma((4,))],
        compiler_params=pltpu.CompilerParams(vmem_limit_bytes=1024 * 1024),
    )(*results)


def solution(mesh):
    return jax.shard_map(
        shards,
        mesh=mesh,
        in_specs=(
            P("dp", "mp"),
            P("dp", "mp"),
            P("dp"),
            P("dp"),
            P("dp"),
            P(),
            P("dp"),
            P("dp", None, "mp"),
            P("dp", None, "mp"),
        ),
        out_specs=(P("dp", "mp"), P("dp", "mp"), P("dp", None, "mp"), P("dp", None, "mp")),
        check_vma=False,
    )
```

time: 80 us -> 76.8 us (0.960)
  Pallas kernels: 78.6 us -> 75 us
    pallas_call x1, Pallas kernels: 3.84 us -> 1.96 us  [shards(): pl.pallas_call(finish, out_shape=shapes, in_specs=[hbm] * 4, out_specs=(h...]
    pallas_call x1, Pallas kernels: 74.8 us -> 73.1 us  [shards(): pl.pallas_call(kernel, out_shape=tuple((pltpu.VMEM(x.shape, bf16) for x i...]
where the time goes in v3:
time: 76.8 us; the launch traced here: 76.5 us
  Pallas kernels  75 us (98%)
  between operations  1.45 us (2%)
    pallas_call x1, Pallas kernels, shards(): pl.pallas_call(kernel, out_shape=tuple((pltpu.VMEM(x.shape, bf16) for x i...  73.1 us
    pallas_call x1, Pallas kernels, shards(): pl.pallas_call(finish, out_shape=shapes, in_specs=[hbm] * 4, out_specs=(h...  1.96 us

profile of v3, /device:TPU:8, one launch (start us, length us, event | category | flops | bytes accessed | tf_op | source)
XLA Modules:
  0.0 76.5 jit_solution(2626053695914453731)
XLA Ops:
  1.3 73.1 %shard_map.120 = (bf16[128,1024]{1,0:T(8,128)(2,1)S(1)}, bf16[128,1024]{1,0:T(8,128)(2,1)S(1)}, bf16[1,6656,128]{2,1,0:T(8,128)(2,1)S(1)}, bf16[1,6656,128]{2,1,0:T(8,128)(2,1)S(1)}) custom-call(s32[4]{0:T(128)} %image_ref.1, s32[32]{0:T(128)} %owner_ref.1, s32[1]{0:T(128)S(6)} %copy.13.tiles_ref, s32[1,128]{1,0:T(1,128)} %bitcast.2, s32[1,128]{1,0:T(1,128)} %bitcast.3, ...), custom_call_target="tpu_custom_call" | custom-call | tf_op jit(solution)/shard_map/pallas_call | solution.py:349
  74.4 2.0 %shard_map.121 = (bf16[128,1024]{1,0:T(8,128)(2,1)}, bf16[128,1024]{1,0:T(8,128)(2,1)}, bf16[1,6656,128]{2,1,0:T(8,128)(2,1)}, bf16[1,6656,128]{2,1,0:T(8,128)(2,1)}) custom-call(bf16[128,1024]{1,0:T(8,128)(2,1)S(1)} %get-tuple-element.8.refs_0_, bf16[128,1024]{1,0:T(8,128)(2,1)S(1)} %get-tuple-element.9.refs_1_, ...), custom_call_target="tpu_custom_call" | custom-call | tf_op jit(solution)/shard_map/pallas_call | solution.py:385

commit v4 on v3

--- a/solution.py
+++ b/solution.py
@@ -62,19 +62,10 @@
     mz, mx = me >> 2, me & 3
 
     def ahead(k):
-        return {"dp": ((mz + (k >> 2)) & 7) * 4 + ((mx + (k & 3)) & 3)}
+        return {"dp": ((mz + k // 4) & 7) * 4 + ((mx + k % 4) & 3)}
 
     def behind(k):
-        return {"dp": ((mz + 8 - (k >> 2)) & 7) * 4 + ((mx + 4 - (k & 3)) & 3)}
-
-    def to_all(send):
-        for k in range(1, 4):
-            send(k)
-
-        @pl.loop(1, 8)
-        def _(dz):
-            for dx in range(4):
-                send(dz * 4 + dx)
+        return {"dp": ((mz + 8 - k // 4) & 7) * 4 + ((mx + 4 - k % 4) & 3)}
 
     nxt = {"dp": (me + 1) & (RANKS - 1)}
     prv = {"dp": (me + RANKS - 1) & (RANKS - 1)}
@@ -121,25 +112,21 @@
     pl.semaphore_wait(entered, 3)
 
     def slab(k):
-        return pl.ds(k * SLAB if isinstance(k, int) else pl.multiple_of(k * SLAB, SLAB), SLAB)
+        return pl.ds(k * SLAB, SLAB)
 
     def send_in(c):
-        def one(k):
+        for k in range(1, RANKS):
             pltpu.make_async_remote_copy(
                 snd.at[c, slab(k)], rcv.at[c, slab(k)], in_send.at[c], in_recv.at[c],
                 device_id=ahead(k), device_id_type=MESH,
             ).start()
 
-        to_all(one)
-
     send_in(0)
-    def one(k):
+    for k in range(1, RANKS):
         pltpu.make_async_remote_copy(
             tab.at[pl.ds(k, 1)], tab_in.at[pl.ds(k, 1)], tab_send, tab_recv,
             device_id=ahead(k), device_id_type=MESH,
         ).start()
-
-    to_all(one)
     for c in range(1, AHEAD):
         fill(c)
         send_in(c)
@@ -204,13 +191,11 @@
         back_copy(c).wait_recv()
         rep[c] = dot(unplace[...], res[c]).astype(bf16)
 
-        def one(k):
+        for k in range(1, RANKS):
             pltpu.make_async_remote_copy(
                 rep.at[c, slab(k)], ret.at[c, slab(k)], out_send.at[c], out_recv.at[c],
                 device_id=behind(k), device_id_type=MESH,
             ).start()
-
-        to_all(one)
 
         ret[c, 0:SLAB] = rep[c, 0:SLAB]
 
@@ -292,18 +277,20 @@
     attend(0, "far", lambda: take_in(1))
     back_copy(0).start()
 
-    @pl.loop(1, CHUNKS)
+    @pl.loop(1, CHUNKS - 1)
     def _(c):
         far_copy(c).wait_recv()
-
-        def between():
-            @pl.when(c < CHUNKS - 1)
-            def _():
-                take_in(c + 1)
-
-        attend(c, "all", between)
+        attend(c, "all", lambda: take_in(c + 1))
         back_copy(c).start()
         send_out(c - 1)
+
+    last = CHUNKS - 1
+    far_copy(last).wait_recv()
+    attend(last, "far")
+    back_copy(last).start()
+    send_out(last - 1)
+    attend(last, "own")
+    send_out(last)
 
     g_t = jnp.transpose(g_low[...].astype(f32)).astype(bf16)
     q_t = jnp.transpose(q_low[...].astype(f32)).astype(bf16)
@@ -311,8 +298,6 @@
         mine = slice(j * STEP, (j + 1) * STEP)
         k_buf[0, mine] = jnp.transpose(dot(q_t, slopes[j])).astype(bf16)
         v_buf[0, mine] = jnp.transpose(dot(g_t, weights[j])).astype(bf16)
-        if j == 0:
-            send_out(CHUNKS - 1)
 
     for c in range(CHUNKS):
         pltpu.make_async_copy(rep.at[c, all_but_first], ret.at[c, all_but_first], out_recv.at[c]).wait()

time: 76.8 us -> 75.4 us (0.982)
  Pallas kernels: 75 us -> 73.9 us
    pallas_call x1, Pallas kernels: 73.1 us -> 71.9 us  [shards(): pl.pallas_call(kernel, out_shape=tuple((pltpu.VMEM(x.shape, bf16) for x i...]
where the time goes in v4:
time: 75.4 us; the launch traced here: 75.3 us
  Pallas kernels  73.9 us (98%)
  between operations  1.47 us (2%)
    pallas_call x1, Pallas kernels, shards(): pl.pallas_call(kernel, out_shape=tuple((pltpu.VMEM(x.shape, bf16) for x i...  71.9 us
    pallas_call x1, Pallas kernels, shards(): pl.pallas_call(finish, out_shape=shapes, in_specs=[hbm] * 4, out_specs=(h...  1.96 us

profile of v4, /device:TPU:8, one launch (start us, length us, event | category | flops | bytes accessed | tf_op | source)
XLA Modules:
  0.0 75.3 jit_solution(3437118810897609805)
XLA Ops:
  1.3 71.9 %shard_map.120 = (bf16[128,1024]{1,0:T(8,128)(2,1)S(1)}, bf16[128,1024]{1,0:T(8,128)(2,1)S(1)}, bf16[1,6656,128]{2,1,0:T(8,128)(2,1)S(1)}, bf16[1,6656,128]{2,1,0:T(8,128)(2,1)S(1)}) custom-call(s32[4]{0:T(128)} %image_ref.1, s32[32]{0:T(128)} %owner_ref.1, s32[1]{0:T(128)S(6)} %copy.13.tiles_ref, s32[1,128]{1,0:T(1,128)} %bitcast.2, s32[1,128]{1,0:T(1,128)} %bitcast.3, ...), custom_call_target="tpu_custom_call" | custom-call | tf_op jit(solution)/shard_map/pallas_call | solution.py:334
  73.2 2.0 %shard_map.121 = (bf16[128,1024]{1,0:T(8,128)(2,1)}, bf16[128,1024]{1,0:T(8,128)(2,1)}, bf16[1,6656,128]{2,1,0:T(8,128)(2,1)}, bf16[1,6656,128]{2,1,0:T(8,128)(2,1)}) custom-call(bf16[128,1024]{1,0:T(8,128)(2,1)S(1)} %get-tuple-element.8.refs_0_, bf16[128,1024]{1,0:T(8,128)(2,1)S(1)} %get-tuple-element.9.refs_1_, ...), custom_call_target="tpu_custom_call" | custom-call | tf_op jit(solution)/shard_map/pallas_call | solution.py:370

commit v5 on v4

--- a/solution.py
+++ b/solution.py
@@ -191,7 +191,7 @@
         back_copy(c).wait_recv()
         rep[c] = dot(unplace[...], res[c]).astype(bf16)
 
-        for k in range(1, RANKS):
+        for k in sorted(range(1, RANKS), key=lambda k: -min(k // 4, 8 - k // 4) - min(k % 4, 4 - k % 4)):
             pltpu.make_async_remote_copy(
                 rep.at[c, slab(k)], ret.at[c, slab(k)], out_send.at[c], out_recv.at[c],
                 device_id=behind(k), device_id_type=MESH,
@@ -235,8 +235,9 @@
 
         def score_step(j, top):
             s = dot(q, k_buf[0, keys_of(j), :], NT)
-            at = iota((1, STEP), 1) + j * STEP
-            valid = (at % TOKP < TILE_TOK) & (at // TOKP < count)
+            at = iota((1, STEP), 1)
+            second = (at >= TOKP).astype(jnp.int32)
+            valid = (at - second * TOKP < TILE_TOK) & (j * (STEP // TOKP) + second < count)
             s = s + jnp.where(valid, 0.0, -1e30)
             scores[j, :n] = s
             return jnp.maximum(top, fold(s, jnp.maximum))

time: 75.4 us -> 76.5 us (1.015)
  Pallas kernels: 73.9 us -> 74.8 us
    pallas_call x1, Pallas kernels: 71.9 us -> 72.9 us  [shards(): pl.pallas_call(kernel, out_shape=tuple((pltpu.VMEM(x.shape, bf16) for x i...]
where the time goes in v5:
time: 76.5 us; the launch traced here: 76.3 us
  Pallas kernels  74.8 us (98%)
  between operations  1.47 us (2%)
    pallas_call x1, Pallas kernels, shards(): pl.pallas_call(kernel, out_shape=tuple((pltpu.VMEM(x.shape, bf16) for x i...  72.9 us
    pallas_call x1, Pallas kernels, shards(): pl.pallas_call(finish, out_shape=shapes, in_specs=[hbm] * 4, out_specs=(h...  1.96 us

profile of v5, /device:TPU:8, one launch (start us, length us, event | category | flops | bytes accessed | tf_op | source)
XLA Modules:
  0.0 76.3 jit_solution(17267017471763956400)
XLA Ops:
  1.3 72.9 %shard_map.120 = (bf16[128,1024]{1,0:T(8,128)(2,1)S(1)}, bf16[128,1024]{1,0:T(8,128)(2,1)S(1)}, bf16[1,6656,128]{2,1,0:T(8,128)(2,1)S(1)}, bf16[1,6656,128]{2,1,0:T(8,128)(2,1)S(1)}) custom-call(s32[4]{0:T(128)} %image_ref.1, s32[32]{0:T(128)} %owner_ref.1, s32[1]{0:T(128)S(6)} %copy.13.tiles_ref, s32[1,128]{1,0:T(1,128)} %bitcast.2, s32[1,128]{1,0:T(1,128)} %bitcast.3, ...), custom_call_target="tpu_custom_call" | custom-call | tf_op jit(solution)/shard_map/pallas_call | solution.py:335
  74.2 2.0 %shard_map.121 = (bf16[128,1024]{1,0:T(8,128)(2,1)}, bf16[128,1024]{1,0:T(8,128)(2,1)}, bf16[1,6656,128]{2,1,0:T(8,128)(2,1)}, bf16[1,6656,128]{2,1,0:T(8,128)(2,1)}) custom-call(bf16[128,1024]{1,0:T(8,128)(2,1)S(1)} %get-tuple-element.8.refs_0_, bf16[128,1024]{1,0:T(8,128)(2,1)S(1)} %get-tuple-element.9.refs_1_, ...), custom_call_target="tpu_custom_call" | custom-call | tf_op jit(solution)/shard_map/pallas_call | solution.py:371
